TPU v7x, 512 devices: a whole 4x4x16 slice. The times are simulated.
512 devices in a mesh: gx: 64 (over z, y), gy: 8 (over x, core).
Axes of the slice: x: 4, y: 4, z: 16, core: 2. Of those that a mesh axis runs over, the one named last changes fastest.
Arguments:
- field: bfloat16 [128, 128, 20, 1024], P('gx', 'gy'), may hold values from -6 to 6
- spectral_weight: bfloat16 [576, 144, 800], P('gx', 'gy'), may hold values from -1 to 1
- skip_weight: bfloat16 [20, 20], replicated, may hold values from -1.25 to 1.25
- skip_bias: float32 [20], replicated, may hold values from -4 to 4
- hidden_weight: bfloat16 [20, 64], replicated, may hold values from -1.25 to 1.25
- hidden_bias: float32 [64], replicated, may hold values from -4 to 4
- out_weight: bfloat16 [64], replicated, may hold values from -0.75 to 0.75
- block_ids: int32 [64, 8, 200], P('gx', 'gy'), may hold values from -1 to 255, as said below
- send_rows: int32 [64, 8, 200], P('gx', 'gy'), may hold values from -1 to 255, as said below
- recv_rows: int32 [64, 8, 100], P('gx', 'gy'), may hold values from 0 to 255, as said below
Outputs:
- saturation: bfloat16 [64, 8, 100, 128], P('gx', 'gy')
Inputs may be any that keep to these rules, and one draw needn't show every extreme that they name: `block_ids`: on each device the listed blocks are distinct local block numbers and fill the first slots; a device lists at most 200 and some device exactly 200; along gx, for each gy index, the lists hold 100 blocks a device on the mean. `send_rows`: -1 exactly where block_ids is -1; distinct on each device; at most 4 blocks of one device go to one owner, and 4 is reached on every draw. `recv_rows`: each owner receives exactly 100 blocks, all from devices with its own gy index; every listed block is named by exactly one slot of its owner.
All inputs are finite; a program needn't handle non-finite values.
Results may differ from a plain program's by a relative error of at most 0.02.
Values may be sent and summed in bfloat16 or wider, within the bound.
A program may use at most 128 MiB of HBM per device.

v0:
```python
import math

import jax
import jax.numpy as jnp
from jax import lax
from jax.sharding import PartitionSpec as P

C = 20
MX = 24
MY = 24
MZ = 12
MT = 12
Z = 32
T_SIZE = 32
TB = 4
CX = 2
CY = 16
NZB = 8


def signed_freqs(kept):
    return jnp.arange(kept, dtype=jnp.int32) - kept // 2


def phase_angles(freqs, places, length):
    turns = places[:, None] * freqs[None, :] % length
    return turns.astype(jnp.float32) * (2.0 * math.pi / length)


def twiddle(places, length, kept, orient, factor):
    theta = phase_angles(signed_freqs(kept), places, length)
    cosine = jnp.cos(theta) * factor
    sine = jnp.sin(theta) * (orient * factor)
    upper = jnp.stack([cosine, sine], axis=-1)
    lower = jnp.stack([-sine, cosine], axis=-1)
    return jnp.stack([upper, lower], axis=1)


def zt_angles(steps):
    places = jnp.arange(steps * Z, dtype=jnp.int32)
    along_z = phase_angles(signed_freqs(MZ), places % Z, Z)
    along_t = phase_angles(signed_freqs(MT), places // Z, T_SIZE)
    return (along_t[:, :, None] + along_z[:, None, :]).reshape(steps * Z, MT * MZ)


def forward_table():
    theta = zt_angles(T_SIZE)
    table = jnp.stack([jnp.cos(theta), -jnp.sin(theta)], axis=1) / math.sqrt(Z * T_SIZE)
    return table.reshape(Z * T_SIZE, 2 * MZ * MT).astype(jnp.bfloat16)


def block_table():
    theta = jnp.transpose(zt_angles(TB))
    table = jnp.stack([jnp.cos(theta), -jnp.sin(theta)], axis=0) / math.sqrt(MX * MY * MZ * MT)
    return table.reshape(2 * MZ * MT, TB * Z).astype(jnp.bfloat16)


def rotate(coeffs, zt_block):
    theta = jnp.repeat(phase_angles(signed_freqs(MT), zt_block * TB, T_SIZE), MZ, axis=1)[
        :, None, :
    ]
    cosine = jnp.cos(theta)
    sine = jnp.sin(theta)
    real_part = coeffs[:, :, 0] * cosine - coeffs[:, :, 1] * sine
    imag_part = coeffs[:, :, 0] * sine + coeffs[:, :, 1] * cosine
    joined = jnp.stack([real_part, imag_part], axis=2).astype(jnp.bfloat16)
    return joined.reshape(coeffs.shape[0], coeffs.shape[1], 2 * MZ * MT)


def block_work(coeff, cells, params, table):
    skip_weight, skip_bias, hidden_weight, hidden_bias, out_weight = params
    spectral = jnp.einsum("bcm,ml->bcl", coeff, table, preferred_element_type=jnp.float32)
    skipped = jnp.einsum("bcl,cd->bdl", cells, skip_weight, preferred_element_type=jnp.float32)
    state = jax.nn.gelu(spectral + skipped + skip_bias[None, :, None]).astype(jnp.bfloat16)
    inner = jnp.einsum("bdl,dh->bhl", state, hidden_weight, preferred_element_type=jnp.float32)
    hidden = jax.nn.gelu(inner + hidden_bias[None, :, None]).astype(jnp.bfloat16)
    return jnp.einsum("bhl,h->bl", hidden, out_weight, preferred_element_type=jnp.float32).astype(
        jnp.bfloat16
    )


def run_blocks(coeff, cells, params):
    table = block_table()
    groups = 4
    member = coeff.shape[0] // groups

    def per_group(packed):
        return block_work(packed[0], packed[1], params, table)

    stacked = (
        coeff.reshape(groups, member, coeff.shape[1], coeff.shape[2]),
        cells.reshape(groups, member, cells.shape[1], cells.shape[2]),
    )
    result = lax.map(per_group, stacked)
    return result.reshape(groups * member, table.shape[1])


def gather_blocks(columns, field, listed):
    safe_ids = jnp.where(listed >= 0, listed, 0)
    column_of = safe_ids // NZB
    zt_block = safe_ids % NZB
    coeff = rotate(columns[column_of].astype(jnp.float32), zt_block)
    blocked = field.reshape(CX * CY, C, NZB, TB * Z)
    cells = blocked[column_of, :, zt_block]
    return (coeff, cells)


def local(
    field,
    spectral_weight,
    skip_weight,
    skip_bias,
    hidden_weight,
    hidden_bias,
    out_weight,
    block_ids,
    send_rows,
    recv_rows,
):
    highest = lax.Precision.HIGHEST
    f32 = jnp.float32
    count_x = lax.axis_size("gx")
    count_y = lax.axis_size("gy")
    kzt = MZ * MT
    part_k = kzt // count_y
    lane_width = C * part_k
    x_first = lax.axis_index("gx") * CX
    y_first = lax.axis_index("gy") * CY
    x_length = CX * count_x
    y_length = CY * count_y
    local_pairs = MX * MY // count_x
    spec_zt = jnp.dot(
        field.reshape(CX * CY * C, Z * T_SIZE), forward_table(), preferred_element_type=jnp.float32
    )
    spec_zt = spec_zt.astype(jnp.bfloat16).reshape(CX, CY, C, 2, count_y, part_k)
    grouped = jnp.transpose(spec_zt, (0, 1, 4, 3, 2, 5)).reshape(CX, CY, count_y, 2 * lane_width)
    spread = lax.all_to_all(grouped, "gy", split_axis=2, concat_axis=1, tiled=True)
    spread = spread.reshape(CX, y_length * 2, lane_width).astype(f32)
    y_whole = twiddle(
        jnp.arange(y_length, dtype=jnp.int32), y_length, MY, -1.0, 1.0 / math.sqrt(y_length)
    )
    y_matrix = jnp.transpose(y_whole, (3, 2, 0, 1)).reshape(2 * MY, 2 * y_length)
    spec_yzt = jnp.einsum("pa,xab->xpb", y_matrix, spread, precision=highest).astype(jnp.bfloat16)
    x_rows = twiddle(
        x_first + jnp.arange(CX, dtype=jnp.int32), x_length, MX, -1.0, 1.0 / math.sqrt(x_length)
    )
    x_matrix = jnp.transpose(x_rows, (2, 3, 0, 1)).reshape(2 * MX, 2 * CX)
    x_data = spec_yzt.astype(f32).reshape(2 * CX, MY * lane_width)
    x_terms = jnp.dot(x_matrix, x_data, precision=highest).reshape(MX, 2, MY, lane_width)
    x_terms = jnp.transpose(x_terms, (0, 2, 1, 3)).reshape(MX * MY, 2, lane_width)
    spec_all = lax.psum_scatter(x_terms, "gx", scatter_dimension=0, tiled=True)
    spec_all = spec_all.reshape(local_pairs, 2, C, part_k)
    weight = spectral_weight.astype(f32).reshape(spectral_weight.shape[0], part_k, 2, C, C)
    real_in = spec_all[:, 0]
    imag_in = spec_all[:, 1]
    mix_real = jnp.einsum(
        "mck,mkcd->mdk", real_in, weight[:, :, 0], precision=highest
    ) - jnp.einsum("mck,mkcd->mdk", imag_in, weight[:, :, 1], precision=highest)
    mix_imag = jnp.einsum(
        "mck,mkcd->mdk", real_in, weight[:, :, 1], precision=highest
    ) + jnp.einsum("mck,mkcd->mdk", imag_in, weight[:, :, 0], precision=highest)
    mixed = (
        jnp.stack([mix_real, mix_imag], axis=1)
        .astype(jnp.bfloat16)
        .reshape(local_pairs, 2 * lane_width)
    )
    gathered = lax.all_gather(mixed, "gx", axis=0, tiled=True).reshape(MX, MY, 2, lane_width)
    x_back = twiddle(x_first + jnp.arange(CX, dtype=jnp.int32), x_length, MX, 1.0, 1.0)
    back_x = jnp.einsum("pqib,xipo->xoqb", gathered.astype(f32), x_back, precision=highest).astype(
        jnp.bfloat16
    )
    back_x = back_x.reshape(CX, 2, MY, C, part_k)
    y_back = twiddle(y_first + jnp.arange(CY, dtype=jnp.int32), y_length, MY, 1.0, 1.0)
    columns = jnp.einsum(
        "xiqck,yiqo->xycok",
        lax.all_gather(back_x, "gy", axis=4, tiled=True).astype(f32),
        y_back,
        precision=highest,
    ).astype(jnp.bfloat16)
    columns = columns.reshape(CX * CY, C, 2, kzt)
    params = (skip_weight, skip_bias, hidden_weight, hidden_bias, out_weight)
    listed = block_ids.reshape(-1)
    targets = send_rows.reshape(-1)
    wanted = recv_rows.reshape(-1)
    capacity = (listed.shape[0] + count_x - 1) // count_x
    landing = jnp.where(targets >= 0, targets, count_x * capacity)
    coeff, cells = gather_blocks(columns, field, listed)
    block_cells = TB * Z
    result = run_blocks(coeff, cells, params)
    outbox = (
        jnp.zeros((count_x * capacity, block_cells), jnp.bfloat16)
        .at[landing]
        .set(result, mode="drop")
    )
    arrived = lax.all_to_all(
        outbox.reshape(count_x, capacity, block_cells),
        "gx",
        split_axis=0,
        concat_axis=0,
        tiled=True,
    )
    saturation = arrived.reshape(count_x * capacity, block_cells)[wanted]
    return saturation.reshape(1, 1, wanted.shape[0], block_cells)


def solution(mesh):
    placed = (
        P("gx", "gy", None, None),
        P("gx", "gy", None),
        P(),
        P(),
        P(),
        P(),
        P(),
        P("gx", "gy", None),
        P("gx", "gy", None),
        P("gx", "gy", None),
    )
    return jax.shard_map(
        local, mesh=mesh, in_specs=placed, out_specs=P("gx", "gy", None, None), check_vma=False
    )
```

profile of v0, /device:TPU:1, one launch (start us, length us, event | category | flops | bytes accessed | tf_op | source)
XLA Modules:
  0.0 601.9 jit_solution(11751924675734937388)
XLA Ops:
  6.7 2.7 add_cosine_fusion
  12.5 2.0 fusion.53
  14.5 6.7 %reshape.1140 = bf16[2,16,20,2,8,18]{2,1,0,5,4,3:T(8,128)(2,1)} reshape(bf16[640,288]{0,1:T(8,128)(2,1)S(1)} %fusion.53) | data formatting | bytes 737280 | tf_op jit(solution)/shard_map/reshape | solution.py:135
  21.2 5.0 copy.72
  26.2 2.4 reshape.1141
  29.4 10.8 %all-to-all-start = ((bf16[2,16,8,720]{3,1,0,2:T(8,128)(2,1)}), bf16[2,16,8,720]{3,1,0,2:T(8,128)(2,1)}, u32[]{:S(2)}, u32[]{:S(2)}) async-start(bf16[2,16,8,720]{3,1,0,2:T(8,128)(2,1)} %copy.73), calls=%async_computation | async-start | bytes 786432 | tf_op jit(solution)/shard_map/all_to_all | solution.py:137
  42.9 3.2 reshape.1147
  53.9 2.0 reshape.1142
  55.9 2.0 fusion.56
  63.4 2.6 copy.80
  70.5 2.6 copy.91
  75.2 4.2 gather_fusion.1
  80.9 252.4 %all-reduce.3.cloned.1.call-done = f32[576,2,360]{2,1,0:T(2,128)} async-done(((f32[576,2,360]{2,1,0:T(2,128)}), f32[576,2,360]{2,1,0:T(2,128)}) %all-reduce.3.cloned.1.call-update) | async-done | bytes 1658896
  334.5 2.5 fusion.49
  337.8 73.9 %all-gather = bf16[64,9,720]{2,1,0:T(8,128)(2,1)S(1)} all-gather(bf16[1,9,720]{2,1,0:T(8,128)(2,1)S(1)} %reshape.1190), channel_id=1, replica_groups=mesh['gx'=64,'gy'=8] {'gx'}, dimensions={0}, use_global_device_ids=true | all-gather | bytes 842400 | tf_op jit(solution)/shard_map/all_gather | solution.py:167
  414.7 54.3 %all_gather.7 = bf16[2,2,24,20,144]{2,1,3,0,4:T(2,128)(2,1)S(1)} all-gather(bf16[2,2,24,20,18]{2,1,3,0,4:T(2,128)(2,1)S(1)} %copy.83), channel_id=1, replica_groups=mesh['gx'=64,'gy'=8] {'gy'}, dimensions={4}, use_global_device_ids=true | all-gather | bytes 622080 | tf_op jit(solution)/shard_map/all_gather | solution.py:176
  469.0 4.8 copy.84
  473.8 1.9 fusion.52
  476.4 15.6 %gather_fusion = bf16[200,20,2,144]{3,2,1,0:T(2,128)(2,1)} fusion(bf16[32,20,2,144]{3,2,1,0:T(2,128)(2,1)S(1)} %copy.86, s32[1024]{0:T(1024)S(1)} %pad_clamp_fusion.1), kind=kCustom, calls=%fused_computation | custom fusion | bytes 4608800 | tf_op jit(solution)/shard_map/gather | solution.py:102
  492.1 8.2 %convert_element_type.193 = f32[200,20,2,144]{3,2,1,0:T(2,128)} convert(bf16[200,20,2,144]{3,2,1,0:T(2,128)(2,1)} %gather_fusion) | non-fusion elementwise | flops 1152000 | bytes 6912000 | tf_op jit(solution)/shard_map/convert_element_type | solution.py:102
  500.3 16.4 %subtract_convert_fusion = (bf16[200,20,1,144]{3,2,1,0:T(2,128)(2,1)}, bf16[200,20,1,144]{3,2,1,0:T(2,128)(2,1)}) fusion(f32[200,20,2,144]{3,2,1,0:T(2,128)} %convert_element_type.193, f32[200,144]{1,0:T(8,128)S(1)} %copy-done.3, f32[200,144]{1,0:T(8,128)S(1)} %copy.87), kind=kLoop, calls=%fused_computation.51 | loop fusion | flops 4608000 | bytes 7142400 | tf_op jit(solution)/shard_map/convert
  516.7 15.0 %pad_maximum_fusion = bf16[200,20,2,144]{3,2,1,0:T(2,128)(2,1)} fusion(bf16[200,20,1,144]{3,2,1,0:T(2,128)(2,1)} %get-tuple-element.131, bf16[200,20,1,144]{3,2,1,0:T(2,128)(2,1)} %get-tuple-element.130), kind=kLoop, calls=%fused_computation.49 | loop fusion | flops 4608000 | bytes 4608000 | tf_op jit(solution)/shard_map/stack | solution.py:66
  531.7 10.2 %reshape.1217 = bf16[4,50,20,288]{3,2,1,0:T(8,128)(2,1)} reshape(bf16[200,20,2,144]{3,2,1,0:T(2,128)(2,1)} %pad_maximum_fusion) | data formatting | bytes 4608000 | tf_op jit(solution)/shard_map/convert_element_type | solution.py:66
  541.9 2.5 copy.92
  544.5 23.1 %while.10 = (s32[]{:T(128)}, bf16[4,50,128]{2,1,0:T(8,128)(2,1)}, bf16[4,50,20,288]{3,1,2,0:T(8,128)(2,1)S(1)}, bf16[288,128]{1,0:T(8,128)(2,1)}, bf16[4,50,20,1...) while((s32[]{:T(128)}, bf16[4,50,128]{2,1,0:T(8,128)(2,1)}, ...), condition=%wide.region_2.3_spmd, body=%wide.region_1.2_spmd.sunk | while | flops 101555200 | bytes 2924817 | solution.py:94
  545.7 2.1 fusion.151
  551.5 2.1 fusion.151
  553.6 1.9 fusion.152
  557.2 2.1 fusion.151
  563.0 2.1 fusion.151
  570.1 9.1 %all-to-all-start.1 = ((bf16[64,4,128]{2,1,0:T(4,128)(2,1)}), bf16[64,4,128]{2,1,0:T(4,128)(2,1)S(1)}, u32[]{:S(2)}, u32[]{:S(2)}) async-start(bf16[64,4,128]{2,1,0:T(4,128)(2,1)} %bitcast.75), calls=%async_computation.1 | async-start | bytes 131072 | tf_op jit(solution)/shard_map/all_to_all | solution.py:195
  579.2 14.1 %all-to-all-done.1 = bf16[64,4,128]{2,1,0:T(4,128)(2,1)S(1)} async-done(((bf16[64,4,128]{2,1,0:T(4,128)(2,1)}), bf16[64,4,128]{2,1,0:T(4,128)(2,1)S(1)}, u32[]{:S(2)}, u32[]{:S(2)}) %all-to-all-start.1) | async-done | bytes 65568 | tf_op jit(solution)/shard_map/all_to_all | solution.py:195
  (126 shorter events, 49.3 us)
Async XLA Ops:
  6.7 3.8 copy-start
  11.2 1.2 copy-start.2
  28.6 12.2 %copy-start.1 = (bf16[2,16,20,1024]{3,1,2,0:T(8,128)(2,1)S(1)}, bf16[2,16,20,1024]{3,1,2,0:T(8,128)(2,1)}, u32[]{:S(2)}) copy-start(bf16[2,16,20,1024]{3,1,2,0:T(8,128)(2,1)} %param.12) | copy-start | bytes 3932164
  29.4 22.6 %all-to-all-start = ((bf16[2,16,8,720]{3,1,0,2:T(8,128)(2,1)}), bf16[2,16,8,720]{3,1,0,2:T(8,128)(2,1)}, u32[]{:S(2)}, u32[]{:S(2)}) async-start(bf16[2,16,8,720]{3,1,0,2:T(8,128)(2,1)} %copy.73), calls=%async_computation | async-start | bytes 786432 | tf_op jit(solution)/shard_map/all_to_all | solution.py:137
  40.3 293.0 %all-reduce.3.cloned.1.call-start = ((), (), s32[]{:S(2)}) async-start(), calls=%async_computation.2 | async-start | bytes 3538944
  41.0 5.2 copy-start.10
  70.5 2.6 copy-start.7
  70.5 4.7 copy-start.11
  73.1 6.4 %copy-start.8 = (f32[2,24,1]{1,2,0:T(1,128)S(1)}, f32[2,24,1]{1,2,0:T(1,128)}, u32[]{:S(2)}) copy-start(f32[2,24,1]{1,2,0:T(1,128)} %get-tuple-element.126) | copy-start | bytes 580
  73.1 6.4 %copy-start.9 = (f32[2,24,1]{1,2,0:T(1,128)S(1)}, f32[2,24,1]{1,2,0:T(1,128)}, u32[]{:S(2)}) copy-start(f32[2,24,1]{1,2,0:T(1,128)} %get-tuple-element.154) | copy-start | bytes 580
  73.1 7.2 %copy-start.4 = (f32[128,144]{0,1:T(8,128)S(1)}, f32[128,144]{0,1:T(8,128)}, u32[]{:S(2)}) copy-start(f32[128,144]{0,1:T(8,128)} %cos.79) | copy-start | bytes 221188
  73.1 7.1 %copy-start.5 = (f32[128,144]{0,1:T(8,128)S(1)}, f32[128,144]{0,1:T(8,128)}, u32[]{:S(2)}) copy-start(f32[128,144]{0,1:T(8,128)} %neg.69) | copy-start | bytes 221188
  73.1 7.8 %copy-start.12 = (s32[1,1,200]{2,1,0:T(1,128)S(1)}, s32[1,1,200]{2,1,0:T(1,128)}, u32[]{:S(2)}) copy-start(s32[1,1,200]{2,1,0:T(1,128)} %param.20) | copy-start | bytes 2404
  469.0 4.8 copy-start.6
  492.1 8.2 %copy-start.3 = (f32[200,144]{1,0:T(8,128)S(1)}, f32[200,144]{1,0:T(8,128)}, u32[]{:S(2)}) copy-start(f32[200,144]{1,0:T(8,128)} %copy.88) | copy-start | bytes 345604
  541.9 2.6 copy-start.13
  541.9 2.6 copy-start.14
  541.9 2.6 copy-start.15
  541.9 2.6 copy-start.16
  544.5 34.7 %copy-start.17 = (s32[1,1,100]{2,1,0:T(1,128)S(1)}, s32[1,1,100]{2,1,0:T(1,128)}, u32[]{:S(2)}) copy-start(s32[1,1,100]{2,1,0:T(1,128)} %param.21) | copy-start | bytes 1204
  570.1 23.3 %all-to-all-start.1 = ((bf16[64,4,128]{2,1,0:T(4,128)(2,1)}), bf16[64,4,128]{2,1,0:T(4,128)(2,1)S(1)}, u32[]{:S(2)}, u32[]{:S(2)}) async-start(bf16[64,4,128]{2,1,0:T(4,128)(2,1)} %bitcast.75), calls=%async_computation.1 | async-start | bytes 131072 | tf_op jit(solution)/shard_map/all_to_all | solution.py:195
Sparse Core Ops, SparseCore 0:
  66.1 267.1 all-reduce.2
where the time goes:
time: 610 us; the launch traced here: 602 us
  waiting for transfers between devices  266 us (44%)
  blocking collectives  128 us (21%)
  local copies, waits for them, and re-layouts  94 us (15%)
  other arithmetic  48.7 us (8%)
  matrix products  28.9 us (5%)
  starting transfers between devices  20.5 us (3%)
  between operations  15 us (2%)
    unnamed x2, waiting for transfers between devices  252 us
    all_gather x1, blocking collectives, local(): lax.all_gather(mixed, 'gx', axis=0, tiled=True)  73.9 us
    all_gather x1, blocking collectives, local(): lax.all_gather(back_x, 'gy', axis=4, tiled=True).astype(f32)  54.3 us
    another operation x1, other arithmetic  16.4 us
    gather x1, local copies, waits for them, and re-layouts, gather_blocks(): coeff = rotate(columns[column_of].astype(jnp.float32), zt_block)  15.6 us
    another operation x1, other arithmetic, rotate(): joined = jnp.stack([real_part, imag_part], axis=2).astype(jnp.bfloat16)  15 us
    all_to_all x1, waiting for transfers between devices, local(): lax.all_to_all(outbox.reshape(count_x, capacity, block_cells), 'gx', spli...  14.1 us
  transfers between devices with their start and end apart: 3, of which 2 were waited for; matrix products, arithmetic and copies ran while one was open for 4% of the time, Pallas kernels for 0%

commit v1 on v0

v1 whole, which is shorter than its diff:
```python
import functools
import math

import jax
import jax.numpy as jnp
import ml_dtypes
import numpy as np
from jax import lax
from jax.experimental import pallas as pl
from jax.experimental.pallas import tpu as pltpu
from jax.sharding import PartitionSpec as P

C = 20
HID = 64
MX = 24
MY = 24
MZ = 12
MT = 12
Z = 32
T_SIZE = 32
X = 128
Y = 128
KZT = MZ * MT
PK = 18
G = 7
R = 8
LW = G * 128
W2 = 2 * C * C
MESH = pl.DeviceIdType.MESH
f32 = jnp.float32
bf16 = jnp.bfloat16
GA = math.sqrt(2.0 / math.pi)
GB = GA * 0.044715


def constants():
    half = ml_dtypes.bfloat16

    def cos_sin(f, n, length):
        a = 2.0 * np.pi * ((f * n) % length) / length
        return np.cos(a), np.sin(a)

    q = np.arange(Z * T_SIZE)
    forward = np.zeros((Z * T_SIZE, 384))
    backward = np.zeros((384, Z * T_SIZE))
    for j in range(R):
        for k in range(PK):
            kk = PK * j + k
            fz, ft = kk % MZ - MZ // 2, kk // MZ - MT // 2
            a = 2.0 * np.pi * (((fz * (q % Z)) % Z) / Z + ((ft * (q // Z)) % T_SIZE) / T_SIZE)
            lane = 128 * (j // 3) + PK * (j % 3) + k
            forward[:, lane] = np.cos(a) / math.sqrt(Z * T_SIZE)
            forward[:, lane + 64] = -np.sin(a) / math.sqrt(Z * T_SIZE)
            backward[lane] = np.cos(a) / math.sqrt(MX * MY * KZT)
            backward[lane + 64] = -np.sin(a) / math.sqrt(MX * MY * KZT)
    fy = np.arange(MY) - MY // 2
    c, s = cos_sin(fy[:, None], np.arange(Y)[None, :], Y)
    y_fwd = np.concatenate([c, s], 0) / math.sqrt(Y)
    y_bwd = np.concatenate([c.T, s.T], 0)
    fx = np.arange(MX) - MX // 2
    x_fwd = np.zeros((R, 48, 16))
    x_bwd = np.zeros((R, 32, 24))
    for e in range(R):
        x = (16 * np.arange(8)[:, None] + 2 * e + np.arange(2)[None, :]).reshape(-1)
        c, s = cos_sin(fx[:, None], x[None, :], X)
        x_fwd[e] = np.concatenate([c, s], 0) / math.sqrt(X)
        x_bwd[e] = np.concatenate([c.T, s.T], 0)
    gather = np.zeros((LW, 128))
    spread = np.zeros((128, LW))
    for ch in range(C):
        for r in range(2):
            for k in range(PK):
                lane = 128 * (ch // 3) + 64 * r + PK * (ch % 3) + k
                gather[lane, 64 * r + ch] = 1.0
                spread[64 * r + ch, lane] = 1.0
    widen = np.zeros((128, LW))
    widen_swapped = np.zeros((128, LW))
    sum_re = np.zeros((LW, 128))
    sum_im = np.zeros((LW, 128))
    for r in range(2):
        for ch in range(C):
            for d in range(C):
                col = 400 * r + C * ch + d
                widen[64 * r + ch, col] = 1.0
                widen_swapped[64 * (1 - r) + ch, col] = 1.0
                sum_re[col, d] = 1.0 - 2.0 * r
                sum_im[col, 64 + d] = 1.0
    regroup = np.zeros((256, 256))
    for e in range(R):
        for zh in range(R):
            for n in range(4):
                regroup[32 * e + 4 * zh + n, 32 * zh + 4 * e + n] = 1.0
    tables = (
        forward, backward, y_fwd, y_bwd, x_fwd, x_bwd, gather, spread,
        widen, widen_swapped, sum_re, sum_im, regroup,
    )
    return [t.astype(half) for t in tables]


def mm(a, b):
    return lax.dot_general(a, b, (((1,), (0,)), ((), ())), preferred_element_type=f32)


def iota(shape, dim):
    return lax.broadcasted_iota(jnp.int32, shape, dim)


def one_hot(mask):
    return jnp.where(mask, 1.0, 0.0).astype(f32)


def twice_gelu(v):
    return v + v * jnp.tanh(v * (GA + GB * (v * v)))


def kernel(*refs):
    (
        field, weight, skip_w, skip_b, hid_w, hid_b, out_w, b_ids, s_rows, r_rows,
        t_fwd, t_bwd, y_fwd, y_bwd, x_fwd, x_bwd, gather, spread,
        widen, widen_sw, sum_re, sum_im, regroup,
        out,
        send_y, recv_y, ya, send_a, recv_a, xa, xb, send_b, recv_b, spec_b, spec_p,
        pairs, amat, mix, mix_p, mix_b, send_c, recv_c, xc, xd, send_d, recv_d, xe, send_e, recv_e,
        s6, part, blk, send_f, recv_f, send_g, recv_g, wpad, perm, pick, idrows, square, skip_k, hid_k,
        skip_col, hid_col, out_col,
        ss_y, rs_y, ss_a, rs_a, ss_b, rs_b, ss_p, rs_p, ls_p, ss_q, rs_q, ls_q, ss_c, rs_c,
        ss_d, rs_d, ss_e, rs_e, ss_f, rs_f, ss_g, rs_g,
    ) = refs
    i = lax.axis_index("gx")
    j = lax.axis_index("gy")
    zh = lax.div(i, R)
    e = lax.rem(i, R)

    def turn(n, d):
        return lax.rem(n + d, R)

    def on_y(d):
        return turn(j, d), (i, turn(j, d))

    def on_z(d):
        return turn(zh, d), (R * turn(zh, d) + e, j)

    def on_e(d):
        return turn(e, d), (R * zh + turn(e, d), j)

    owners = []
    for n in range(3):
        first = MY * (3 * e + n) + 3 * zh
        owners.append((lax.div(first, 9), lax.div(lax.rem(first, 9), 3)))
    sources = []
    for a in range(3):
        first = 9 * i + 3 * a
        jx, jy = lax.div(first, MY), lax.rem(first, MY)
        sources.append((R * lax.div(jy, 3) + lax.div(jx, 3), lax.rem(jx, 3)))

    barrier = pltpu.get_barrier_semaphore()
    for near in (on_y, on_z, on_e):
        for d in range(1, R):
            pl.semaphore_signal(barrier, inc=1, device_id=near(d)[1], device_id_type=MESH)
    for other, _ in owners + sources:

        @pl.when(other != i)
        def _():
            pl.semaphore_signal(barrier, inc=1, device_id=(other, j), device_id_type=MESH)

    def exchange_copies(near, me, send, recv, send_sem, recv_sem, same=False):
        copies = []
        for d in range(1, R):
            peer, device = near(d)
            copies.append(
                pltpu.make_async_remote_copy(
                    src_ref=send if same else send.at[peer],
                    dst_ref=recv.at[me],
                    send_sem=send_sem.at[d - 1],
                    recv_sem=recv_sem.at[d - 1],
                    device_id=device,
                    device_id_type=MESH,
                )
            )
        return copies

    def exchange(near, me, send, recv, send_sem, recv_sem, same=False, beside=None):
        copies = exchange_copies(near, me, send, recv, send_sem, recv_sem, same)
        for copy in copies:
            copy.start()
        recv[me] = send[...] if same else send[me]
        if beside is not None:
            beside()
        for copy in copies:
            copy.wait()

    lane = iota((1, 128), 1)
    in_half = lane & 63
    piece = [
        (in_half >= PK * m) & (in_half < PK * (m + 1)) for m in range(3)
    ]
    fwd_sign = jnp.where(lane < 64, 1.0, -1.0)

    def regrouped(held, n):
        total = jnp.zeros(held[0].shape, f32)
        for m, rows in enumerate(held):
            if rows is None:
                continue
            shift = (PK * (m - n)) % 128
            moved = rows if shift == 0 else pltpu.roll(rows, shift, 1)
            total = jnp.where(piece[m], moved, total)
        return total

    def combine(cosines, sines, sign):
        return cosines + sign * pltpu.roll(sines, 64, 1)

    for x in range(2):
        got = mm(field[320 * x : 320 * x + 320, :], t_fwd[...])
        for g in range(G):
            for t in range(3):
                held = [
                    got[16 * c : 16 * c + 16, 128 * t : 128 * t + 128] if c < C else None
                    for c in range(3 * g, 3 * g + 3)
                ]
                for n in range(min(3, R - 3 * t)):
                    send_y[3 * t + n, 16 * x : 16 * x + 16, 128 * g : 128 * g + 128] = (
                        regrouped(held, n).astype(bf16)
                    )

    expected = 3 * (R - 1)
    for other, _ in owners + sources:
        expected = expected + jnp.where(other != i, 1, 0)
    pl.semaphore_wait(barrier, expected)

    def prepare():
        wpad[...] = jnp.zeros((288, LW), bf16)
        for p in range(9):
            wpad[32 * p : 32 * p + PK, 0:W2] = weight[p]
        ya[...] = jnp.zeros((384, 128), f32)
        xb[...] = jnp.zeros((576, 128), f32)
        xd[...] = jnp.zeros((384, 128), f32)
        mix[...] = jnp.zeros((72, 128), f32)
        idrows[...] = jnp.full((8, 256), -1, jnp.int32)
        idrows[0:1, 0:200] = b_ids[...]
        idrows[1:2, 0:200] = s_rows[...]
        idrows[2:3, 0:100] = r_rows[...]
        row = iota((256, 256), 0)
        by_block = one_hot(row == idrows[0:1, :]).astype(bf16)
        by_row = one_hot(row == idrows[1:2, :]).astype(bf16)
        perm[...] = lax.dot_general(
            by_row, by_block, (((1,), (1,)), ((), ())), preferred_element_type=f32
        ).astype(bf16)
        place = iota((256, 128), 0)
        name = ((place >> 2) & 7) * 32 + (place >> 5) * 4 + (place & 3)
        pick[...] = one_hot(name == idrows[2:3, 0:128]).T.astype(bf16)
        def spread_map(values, rows, cols, places):
            shift = places.bit_length() - 1
            left = one_hot((iota((rows, 128), 0) >> shift) == iota((rows, 128), 1)).astype(bf16)
            right = one_hot((iota((128, cols), 1) >> shift) == iota((128, cols), 0)).astype(bf16)
            wide = mm(mm(left, values.T.astype(bf16)).astype(bf16), right)
            same = (iota((rows, cols), 0) & (places - 1)) == (iota((rows, cols), 1) & (places - 1))
            return jnp.where(same, wide, 0.0).astype(bf16)

        square[...] = jnp.zeros((128, 128), f32)
        square[0:C, 0:C] = skip_w[...].astype(f32)
        skip_k[...] = spread_map(square[...], 320, 320, 16)
        square[0:C, 0:HID] = hid_w[...].astype(f32)
        hid_k[...] = spread_map(square[...], 512, 160, 8)

        def column(values, places, width, rows):
            shift = places.bit_length() - 1
            at = one_hot((iota((rows, width), 0) >> shift) == iota((rows, width), 1))
            return jnp.broadcast_to(
                jnp.sum(at * values, axis=1, keepdims=True), (rows, 256)
            )

        skip_col[...] = column(skip_b[...], 16, C, 320)
        hid_col[...] = column(hid_b[...], 8, HID, 512)
        out_col[...] = column(0.5 * out_w[...].astype(f32), 8, HID, 512)

    exchange(on_y, j, send_y, recv_y, ss_y, rs_y, beside=prepare)

    for x in range(2):
        data = recv_y[:, 16 * x : 16 * x + 16, :].reshape(Y, LW)
        got = mm(y_fwd[...], data)
        for g in range(G):
            part_g = got[:, 128 * g : 128 * g + 128]
            ya[pl.ds(192 * x + g, MY, stride=8), :] = combine(
                part_g[0:MY], part_g[MY : 2 * MY], fwd_sign
            )
    for p in range(R):
        send_a[p] = jnp.concatenate(
            [ya[24 * p : 24 * p + 24, :], ya[192 + 24 * p : 216 + 24 * p, :]], axis=0
        ).astype(bf16)
    exchange(on_z, zh, send_a, recv_a, ss_a, rs_a)

    for p in range(R):
        xa[48 * p : 48 * p + 48, :] = recv_a[p].astype(f32)
    used = [8 * a + g for a in range(3) for g in range(G)]
    data = jnp.concatenate(
        [xa[pl.ds(u, 16, stride=24), :] for u in used], axis=1
    ).astype(bf16)
    got = mm(x_fwd[e], data)
    for n, u in enumerate(used):
        part_u = got[:, 128 * n : 128 * n + 128]
        xb[pl.ds(u, MX, stride=24), :] = combine(part_u[0:MX], part_u[MX : 2 * MX], fwd_sign)
    for p in range(R):
        send_b[p] = jnp.concatenate(
            [xb[72 * p : 72 * p + 72, :], jnp.zeros((8, 128), f32)], axis=0
        ).astype(bf16)
    exchange(on_e, e, send_b, recv_b, ss_b, rs_b)
    total = recv_b[0].astype(f32)
    for p in range(1, R):
        total = total + recv_b[p].astype(f32)
    for n in range(3):
        spec_b[n] = total[24 * n : 24 * n + 24]

    def own_copy(src, n, dst, a, send_sem, recv_sem, device):
        return pltpu.make_async_remote_copy(
            src_ref=src.at[n],
            dst_ref=dst.at[a],
            send_sem=send_sem.at[n],
            recv_sem=recv_sem.at[a],
            device_id=(device, j),
            device_id_type=MESH,
        )

    def hand_over(src, dst, targets, origins, send_sem, recv_sem, local_sem):
        for n, (device, a) in enumerate(targets):

            @pl.when(device != i)
            def _():
                own_copy(src, n, dst, a, send_sem, recv_sem, device).start()

            @pl.when(device == i)
            def _():
                copy = pltpu.make_async_copy(src.at[n], dst.at[a], local_sem.at[n])
                copy.start()
                copy.wait()

        for n, (device, a) in enumerate(targets):

            @pl.when(device != i)
            def _():
                own_copy(src, n, dst, a, send_sem, recv_sem, device).wait_send()

        for a, (device, n) in enumerate(origins):

            @pl.when(device != i)
            def _():
                own_copy(src, n, dst, a, send_sem, recv_sem, device).wait_recv()

    hand_over(spec_b, spec_p, owners, sources, ss_p, rs_p, ls_p)

    own_k = one_hot(
        (iota((32, 128), 1) & 63 < 3 * PK)
        & (lax.rem(iota((32, 128), 1) & 63, PK) == iota((32, 128), 0))
    )
    for n in range(3):
        pairs[24 * n : 24 * n + 24, :] = spec_p[n]
    for p in range(9):
        for g in range(G):
            row = jnp.broadcast_to(pairs[8 * p + g : 8 * p + g + 1, :], (32, 128))
            amat[32 * p : 32 * p + 32, 128 * g : 128 * g + 128] = (row * own_k).astype(bf16)
    compact = mm(amat[...], gather[...]).astype(bf16)
    weights = wpad[...].astype(f32)
    straight = (mm(compact, widen[...]) * weights).astype(bf16)
    crossed = (mm(compact, widen_sw[...]) * weights).astype(bf16)
    mixed = (mm(straight, sum_re[...]) + mm(crossed, sum_im[...])).astype(bf16)
    wide = mm(mixed, spread[...])
    for p in range(9):
        for g in range(G):
            tile = wide[32 * p : 32 * p + 32, 128 * g : 128 * g + 128] * own_k
            mix[8 * p + g : 8 * p + g + 1, :] = jnp.sum(tile, axis=0, keepdims=True)
    for a in range(3):
        mix_p[a] = mix[24 * a : 24 * a + 24, :]

    hand_over(mix_p, mix_b, sources, owners, ss_q, rs_q, ls_q)
    send_c[...] = jnp.concatenate(
        [mix_b[0], mix_b[1], mix_b[2], jnp.zeros((8, 128), f32)], axis=0
    ).astype(bf16)
    exchange(on_e, e, send_c, recv_c, ss_c, rs_c, same=True)

    for p in range(R):
        xc[72 * p : 72 * p + 72, :] = recv_c[p].astype(f32)[0:72]
    data = jnp.concatenate(
        [xc[pl.ds(u, MX, stride=24), :] for u in used], axis=1
    ).astype(bf16)
    got = mm(x_bwd[e], data)
    for n, u in enumerate(used):
        part_u = got[:, 128 * n : 128 * n + 128]
        xd[pl.ds(u, 16, stride=24), :] = combine(part_u[0:16], part_u[16:32], -fwd_sign)
    for p in range(R):
        send_d[p] = xd[48 * p : 48 * p + 48, :].astype(bf16)
    exchange(on_z, zh, send_d, recv_d, ss_d, rs_d)

    for p in range(R):
        got = recv_d[p].astype(f32)
        xe[24 * p : 24 * p + 24, :] = got[0:24]
        xe[192 + 24 * p : 216 + 24 * p, :] = got[24:48]
    for x in range(2):
        data = jnp.concatenate(
            [xe[pl.ds(192 * x + g, MY, stride=8), :] for g in range(G)], axis=1
        ).astype(bf16)
        got = mm(y_bwd[...], data)
        for g in range(G):
            part_g = got[:, 128 * g : 128 * g + 128]
            turned = combine(part_g[0:Y], part_g[Y : 2 * Y], -fwd_sign).astype(bf16)
            send_e[:, 16 * x : 16 * x + 16, 128 * g : 128 * g + 128] = turned.reshape(R, 16, 128)
    exchange(on_y, j, send_e, recv_e, ss_e, rs_e)

    for t in range(3):
        for g in range(G):
            held = [
                recv_e[n, :, 128 * g : 128 * g + 128].astype(f32) if n < R else None
                for n in range(3 * t, 3 * t + 3)
            ]
            for m in range(min(3, C - 3 * g)):
                total = regrouped(held, m).astype(bf16)
                for x in range(2):
                    row = 320 * x + 16 * (3 * g + m)
                    s6[row : row + 16, 128 * t : 128 * t + 128] = total[16 * x : 16 * x + 16]

    @pl.loop(0, 2)
    def _(x):
        rows = pl.ds(pl.multiple_of(x * 320, 320), 320)
        for c in range(4):
            cut = slice(256 * c, 256 * c + 256)
            value = mm(s6[rows, :], t_bwd[:, cut]) + mm(skip_k[...], field[rows, cut])
            state = 0.5 * twice_gelu(value + skip_col[...])
            halves = state.reshape(C, 2, 8, 256)
            for h in range(2):
                inner = mm(hid_k[...], halves[:, h].reshape(160, 256).astype(bf16))
                weighed = twice_gelu(inner + hid_col[...]) * out_col[...]
                part[pl.ds(pl.multiple_of(x * 16, 16) + 8 * h, 8), cut] = jnp.sum(
                    weighed.reshape(HID, 8, 256), axis=0
                )

    for b in range(8):
        blk[pl.ds(b, 32, stride=8), :] = part[:, 128 * b : 128 * b + 128]

    send_f[...] = mm(perm[...], blk[...].astype(bf16)).astype(bf16).reshape(R, 32, 128)
    exchange(on_z, zh, send_f, recv_f, ss_f, rs_f)
    send_g[...] = mm(regroup[...], recv_f[...].reshape(256, 128)).astype(bf16).reshape(R, 32, 128)
    exchange(on_e, e, send_g, recv_g, ss_g, rs_g)
    owned = mm(pick[...], recv_g[...].reshape(256, 128))
    out[...] = owned[0:100].astype(bf16)


def scratch():
    v = pltpu.VMEM
    dma = pltpu.SemaphoreType.DMA
    buffers = [
        v((R, 32, LW), bf16),
        v((R, 32, LW), bf16),
        v((384, 128), f32),
        v((R, 48, 128), bf16),
        v((R, 48, 128), bf16),
        v((384, 128), f32),
        v((576, 128), f32),
        v((R, 80, 128), bf16),
        v((R, 80, 128), bf16),
        v((3, 24, 128), f32),
        v((3, 24, 128), f32),
        v((72, 128), f32),
        v((288, LW), bf16),
        v((72, 128), f32),
        v((3, 24, 128), f32),
        v((3, 24, 128), f32),
        v((80, 128), bf16),
        v((R, 80, 128), bf16),
        v((576, 128), f32),
        v((384, 128), f32),
        v((R, 48, 128), bf16),
        v((R, 48, 128), bf16),
        v((384, 128), f32),
        v((R, 32, LW), bf16),
        v((R, 32, LW), bf16),
        v((640, 384), bf16),
        v((32, 1024), f32),
        v((256, 128), f32),
        v((R, 32, 128), bf16),
        v((R, 32, 128), bf16),
        v((R, 32, 128), bf16),
        v((R, 32, 128), bf16),
        v((288, LW), bf16),
        v((256, 256), bf16),
        v((128, 256), bf16),
        v((8, 256), jnp.int32),
        v((128, 128), f32),
        v((320, 320), bf16),
        v((512, 160), bf16),
        v((320, 256), f32),
        v((512, 256), f32),
        v((512, 256), f32),
    ]
    sems = []
    for count in (7, 7, 7, 7, 7, 7, 3, 3, 3, 3, 3, 3, 7, 7, 7, 7, 7, 7, 7, 7, 7, 7):
        sems.append(dma((count,)))
    return buffers + sems


def local(
    field,
    spectral_weight,
    skip_weight,
    skip_bias,
    hidden_weight,
    hidden_bias,
    out_weight,
    block_ids,
    send_rows,
    recv_rows,
):
    tables = [jnp.asarray(t) for t in constants()]
    args = [
        jnp.transpose(field, (0, 2, 1, 3)).reshape(640, Z * T_SIZE),
        spectral_weight,
        skip_weight,
        skip_bias.reshape(1, C),
        hidden_weight,
        hidden_bias.reshape(1, HID),
        out_weight.reshape(1, HID),
        block_ids.reshape(1, 200),
        send_rows.reshape(1, 200),
        recv_rows.reshape(1, 100),
    ] + tables
    vmem = pl.BlockSpec(memory_space=pltpu.VMEM)
    result = pl.pallas_call(
        kernel,
        out_shape=jax.ShapeDtypeStruct((100, 128), bf16),
        in_specs=[vmem] * len(args),
        out_specs=vmem,
        scratch_shapes=scratch(),
        compiler_params=pltpu.CompilerParams(
            collective_id=0, has_side_effects=True, vmem_limit_bytes=56 * 1024 * 1024
        ),
    )(*args)
    return result.reshape(1, 1, 100, 128)


def solution(mesh):
    placed = (
        P("gx", "gy", None, None),
        P("gx", "gy", None),
        P(),
        P(),
        P(),
        P(),
        P(),
        P("gx", "gy", None),
        P("gx", "gy", None),
        P("gx", "gy", None),
    )
    return jax.shard_map(
        local, mesh=mesh, in_specs=placed, out_specs=P("gx", "gy", None, None), check_vma=False
    )
```

time: 610 us -> 97.5 us (0.16); the launches traced: 602 us -> 97 us
  waiting for transfers between devices: 266 us -> 0 us
  blocking collectives: 128 us -> 0 us
  Pallas kernels: 0 us -> 95.7 us
  local copies, waits for them, and re-layouts: 94 us -> 1.35 us
  other arithmetic: 48.7 us -> 0 us
  matrix products: 28.9 us -> 0 us
  starting transfers between devices: 20.5 us -> 0 us
  between operations: 15 us -> 0.01 us
    unnamed x2 -> x0, waiting for transfers between devices: 252 us -> none
    all_gather x2 -> x0, blocking collectives: 128 us -> none  [the longest x1 73.9 us: local(): lax.all_gather(mixed, 'gx', axis=0, tiled=True)]
    pallas_call x0 -> x1, Pallas kernels: none -> 95.7 us  [local(): pl.pallas_call(kernel, out_shape=jax.ShapeDtypeStruct((100, 128), bf16),...]
    reshape x17 -> x0, local copies, waits for them, and re-layouts: 33 us -> none  [the longest x2 11.7 us: local(): spec_zt.astype(jnp.bfloat16).reshape(CX, CY, C, 2, count_y, part_k)]
    another operation x9 -> x0, other arithmetic: 32.1 us -> none
    dot_general x17 -> x0, matrix products: 28.9 us -> none  [the longest x4 8.39 us: block_work(): jnp.einsum('bcm,ml->bcl', coeff, table, preferred_element_type=jnp.float32)]
    gather x3 -> x0, local copies, waits for them, and re-layouts: 21.1 us -> none  [the longest x1 15.6 us: gather_blocks(): coeff = rotate(columns[column_of].astype(jnp.float32), zt_block)]
    all_to_all x2 -> x0, starting transfers between devices: 20 us -> none  [the longest x1 10.8 us: local(): lax.all_to_all(grouped, 'gy', split_axis=2, concat_axis=1, tiled=True)]
  transfers between devices with their start and end apart: 3 -> 0, of which waited for: 2 -> 0; matrix products, arithmetic and copies ran while one was open for 4% -> 0% of each run, Pallas kernels for 0% -> 0%
where the time goes in v1:
time: 97.5 us; the launch traced here: 97 us
  Pallas kernels  95.7 us (98%)
  local copies, waits for them, and re-layouts  1.35 us (1%)
    pallas_call x1, Pallas kernels, local(): pl.pallas_call(kernel, out_shape=jax.ShapeDtypeStruct((100, 128), bf16),...  95.7 us

profile of v1, /device:TPU:1, one launch (start us, length us, event | category | flops | bytes accessed | tf_op | source)
XLA Modules:
  0.0 97.0 jit_solution(13221736529227379375)
XLA Ops:
  0.0 95.7 %shard_map.217 = bf16[100,128]{1,0:T(8,128)(2,1)} custom-call(bf16[640,1024]{1,0:T(8,128)(2,1)} %bitcast.10, bf16[9,18,800]{2,1,0:T(8,128)(2,1)} %refs_1_.1, bf16[20,20]{1,0:T(8,128)(2,1)} %refs_2_.1, f32[1,20]{1,0:T(1,128)} %bitcast.14, bf16[20,64]{1,0:T(8,128)(2,1)} %refs_4_.1, f32[1,64]{1,0:T(1,128)} %bitcast.15, bf16[1,64]{1,0:T(2,128)(2,1)} %bitcast.16, ...), custom_call_target="tpu_custom_call" | custom-call | tf_op jit(solution)/shard_map/pallas_call | solution.py:524
  95.7 1.4 %copy.25 = bf16[1,1,100,128]{3,2,1,0:T(8,128)(2,1)} copy(bf16[1,1,100,128]{3,2,1,0:T(8,128)(2,1)} %bitcast.11) | data formatting | bytes 51200

commit v2 on v1

--- a/solution.py
+++ b/solution.py
@@ -115,14 +115,17 @@
 
 def kernel(*refs):
     (
-        field, weight, skip_w, skip_b, hid_w, hid_b, out_w, b_ids, s_rows, r_rows,
-        t_fwd, t_bwd, y_fwd, y_bwd, x_fwd, x_bwd, gather, spread,
+        field_in, weight_in, skip_w, skip_b, hid_w, hid_b, out_w, b_ids, s_rows, r_rows,
+        t_fwd_in, t_bwd_in, y_fwd_in, y_bwd_in, x_fwd_in, x_bwd_in, gather_in, spread_in,
+        widen_in, widen_sw_in, sum_re_in, sum_im_in, regroup_in,
+        out,
+        field, weight, t_fwd, t_bwd, y_fwd, y_bwd, x_fwd, x_bwd, gather, spread,
         widen, widen_sw, sum_re, sum_im, regroup,
-        out,
         send_y, recv_y, ya, send_a, recv_a, xa, xb, send_b, recv_b, spec_b, spec_p,
         pairs, amat, mix, mix_p, mix_b, send_c, recv_c, xc, xd, send_d, recv_d, xe, send_e, recv_e,
         s6, part, blk, send_f, recv_f, send_g, recv_g, wpad, perm, pick, idrows, square, skip_k, hid_k,
         skip_col, hid_col, out_col,
+        fetched,
         ss_y, rs_y, ss_a, rs_a, ss_b, rs_b, ss_p, rs_p, ls_p, ss_q, rs_q, ls_q, ss_c, rs_c,
         ss_d, rs_d, ss_e, rs_e, ss_f, rs_f, ss_g, rs_g,
     ) = refs
@@ -163,14 +166,26 @@
         def _():
             pl.semaphore_signal(barrier, inc=1, device_id=(other, j), device_id_type=MESH)
 
+    fetch = []
+    wanted = [
+        (field_in.at[0], field.at[0]), (t_fwd_in, t_fwd), (field_in.at[1], field.at[1]),
+        (y_fwd_in, y_fwd), (weight_in, weight), (x_fwd_in, x_fwd), (gather_in, gather),
+        (widen_in, widen), (widen_sw_in, widen_sw), (sum_re_in, sum_re), (sum_im_in, sum_im),
+        (spread_in, spread), (x_bwd_in, x_bwd), (y_bwd_in, y_bwd), (t_bwd_in, t_bwd),
+        (regroup_in, regroup),
+    ]
+    for n, (source, target) in enumerate(wanted):
+        fetch.append(pltpu.make_async_copy(source, target, fetched.at[n]))
+        fetch[n].start()
+
     def exchange_copies(near, me, send, recv, send_sem, recv_sem, same=False):
         copies = []
         for d in range(1, R):
             peer, device = near(d)
             copies.append(
                 pltpu.make_async_remote_copy(
-                    src_ref=send if same else send.at[peer],
-                    dst_ref=recv.at[me],
+                    src_ref=send if same else send(peer),
+                    dst_ref=recv(me),
                     send_sem=send_sem.at[d - 1],
                     recv_sem=recv_sem.at[d - 1],
                     device_id=device,
@@ -179,15 +194,32 @@
             )
         return copies
 
-    def exchange(near, me, send, recv, send_sem, recv_sem, same=False, beside=None):
-        copies = exchange_copies(near, me, send, recv, send_sem, recv_sem, same)
+    def start(copies):
         for copy in copies:
             copy.start()
-        recv[me] = send[...] if same else send[me]
-        if beside is not None:
-            beside()
+
+    def finish(copies):
         for copy in copies:
             copy.wait()
+
+    def exchange(near, me, send, recv, send_sem, recv_sem, same=False):
+        copies = exchange_copies(
+            near, me, send if same else lambda p: send.at[p], lambda p: recv.at[p],
+            send_sem, recv_sem, same,
+        )
+        start(copies)
+        recv[me] = send[...] if same else send[me]
+        finish(copies)
+
+    def copies_y(x, send, recv, send_sem, recv_sem):
+        return exchange_copies(
+            on_y, j, lambda p: send.at[p, x], lambda p: recv.at[x, p], send_sem.at[x], recv_sem.at[x]
+        )
+
+    def copies_z(x, send, recv, send_sem, recv_sem):
+        return exchange_copies(
+            on_z, zh, lambda p: send.at[p, x], lambda p: recv.at[p, x], send_sem.at[x], recv_sem.at[x]
+        )
 
     lane = iota((1, 128), 1)
     in_half = lane & 63
@@ -209,8 +241,8 @@
     def combine(cosines, sines, sign):
         return cosines + sign * pltpu.roll(sines, 64, 1)
 
-    for x in range(2):
-        got = mm(field[320 * x : 320 * x + 320, :], t_fwd[...])
+    def along_zt(x):
+        got = mm(field[x], t_fwd[...])
         for g in range(G):
             for t in range(3):
                 held = [
@@ -218,14 +250,28 @@
                     for c in range(3 * g, 3 * g + 3)
                 ]
                 for n in range(min(3, R - 3 * t)):
-                    send_y[3 * t + n, 16 * x : 16 * x + 16, 128 * g : 128 * g + 128] = (
+                    send_y[3 * t + n, x, :, 128 * g : 128 * g + 128] = (
                         regrouped(held, n).astype(bf16)
                     )
+
+    fetch[0].wait()
+    fetch[1].wait()
+    along_zt(0)
 
     expected = 3 * (R - 1)
     for other, _ in owners + sources:
         expected = expected + jnp.where(other != i, 1, 0)
     pl.semaphore_wait(barrier, expected)
+
+    going_y = [copies_y(x, send_y, recv_y, ss_y, rs_y) for x in range(2)]
+    start(going_y[0])
+    fetch[2].wait()
+    along_zt(1)
+    start(going_y[1])
+    for x in range(2):
+        recv_y[x, j] = send_y[j, x]
+    for copy in fetch[3:]:
+        copy.wait()
 
     def prepare():
         wpad[...] = jnp.zeros((288, LW), bf16)
@@ -273,24 +319,25 @@
         hid_col[...] = column(hid_b[...], 8, HID, 512)
         out_col[...] = column(0.5 * out_w[...].astype(f32), 8, HID, 512)
 
-    exchange(on_y, j, send_y, recv_y, ss_y, rs_y, beside=prepare)
-
+    prepare()
+
+    going_a = [copies_z(x, send_a, recv_a, ss_a, rs_a) for x in range(2)]
     for x in range(2):
-        data = recv_y[:, 16 * x : 16 * x + 16, :].reshape(Y, LW)
-        got = mm(y_fwd[...], data)
+        finish(going_y[x])
+        got = mm(y_fwd[...], recv_y[x].reshape(Y, LW))
         for g in range(G):
             part_g = got[:, 128 * g : 128 * g + 128]
             ya[pl.ds(192 * x + g, MY, stride=8), :] = combine(
                 part_g[0:MY], part_g[MY : 2 * MY], fwd_sign
             )
+        send_a[:, x] = ya[192 * x : 192 * x + 192, :].astype(bf16).reshape(R, 24, 128)
+        start(going_a[x])
+        recv_a[zh, x] = send_a[zh, x]
+    finish(going_a[0])
+    finish(going_a[1])
+
     for p in range(R):
-        send_a[p] = jnp.concatenate(
-            [ya[24 * p : 24 * p + 24, :], ya[192 + 24 * p : 216 + 24 * p, :]], axis=0
-        ).astype(bf16)
-    exchange(on_z, zh, send_a, recv_a, ss_a, rs_a)
-
-    for p in range(R):
-        xa[48 * p : 48 * p + 48, :] = recv_a[p].astype(f32)
+        xa[48 * p : 48 * p + 48, :] = recv_a[p].astype(f32).reshape(48, 128)
     used = [8 * a + g for a in range(3) for g in range(G)]
     data = jnp.concatenate(
         [xa[pl.ds(u, 16, stride=24), :] for u in used], axis=1
@@ -385,15 +432,18 @@
     for n, u in enumerate(used):
         part_u = got[:, 128 * n : 128 * n + 128]
         xd[pl.ds(u, 16, stride=24), :] = combine(part_u[0:16], part_u[16:32], -fwd_sign)
-    for p in range(R):
-        send_d[p] = xd[48 * p : 48 * p + 48, :].astype(bf16)
-    exchange(on_z, zh, send_d, recv_d, ss_d, rs_d)
-
-    for p in range(R):
-        got = recv_d[p].astype(f32)
-        xe[24 * p : 24 * p + 24, :] = got[0:24]
-        xe[192 + 24 * p : 216 + 24 * p, :] = got[24:48]
+    going_d = [copies_z(x, send_d, recv_d, ss_d, rs_d) for x in range(2)]
     for x in range(2):
+        for p in range(R):
+            send_d[p, x] = xd[48 * p + 24 * x : 48 * p + 24 * x + 24, :].astype(bf16)
+        start(going_d[x])
+        recv_d[zh, x] = send_d[zh, x]
+
+    going_e = [copies_y(x, send_e, recv_e, ss_e, rs_e) for x in range(2)]
+    for x in range(2):
+        finish(going_d[x])
+        for p in range(R):
+            xe[192 * x + 24 * p : 192 * x + 24 * p + 24, :] = recv_d[p, x].astype(f32)
         data = jnp.concatenate(
             [xe[pl.ds(192 * x + g, MY, stride=8), :] for g in range(G)], axis=1
         ).astype(bf16)
@@ -401,27 +451,25 @@
         for g in range(G):
             part_g = got[:, 128 * g : 128 * g + 128]
             turned = combine(part_g[0:Y], part_g[Y : 2 * Y], -fwd_sign).astype(bf16)
-            send_e[:, 16 * x : 16 * x + 16, 128 * g : 128 * g + 128] = turned.reshape(R, 16, 128)
-    exchange(on_y, j, send_e, recv_e, ss_e, rs_e)
-
-    for t in range(3):
-        for g in range(G):
-            held = [
-                recv_e[n, :, 128 * g : 128 * g + 128].astype(f32) if n < R else None
-                for n in range(3 * t, 3 * t + 3)
-            ]
-            for m in range(min(3, C - 3 * g)):
-                total = regrouped(held, m).astype(bf16)
-                for x in range(2):
-                    row = 320 * x + 16 * (3 * g + m)
-                    s6[row : row + 16, 128 * t : 128 * t + 128] = total[16 * x : 16 * x + 16]
+            send_e[:, x, :, 128 * g : 128 * g + 128] = turned.reshape(R, 16, 128)
+        start(going_e[x])
+        recv_e[x, j] = send_e[j, x]
 
     @pl.loop(0, 2)
     def _(x):
-        rows = pl.ds(pl.multiple_of(x * 320, 320), 320)
+        finish(copies_y(x, send_e, recv_e, ss_e, rs_e))
+        for t in range(3):
+            for g in range(G):
+                held = [
+                    recv_e[x, n, :, 128 * g : 128 * g + 128].astype(f32) if n < R else None
+                    for n in range(3 * t, 3 * t + 3)
+                ]
+                for m in range(min(3, C - 3 * g)):
+                    row = 16 * (3 * g + m)
+                    s6[row : row + 16, 128 * t : 128 * t + 128] = regrouped(held, m).astype(bf16)
         for c in range(4):
             cut = slice(256 * c, 256 * c + 256)
-            value = mm(s6[rows, :], t_bwd[:, cut]) + mm(skip_k[...], field[rows, cut])
+            value = mm(s6[...], t_bwd[:, cut]) + mm(skip_k[...], field[x, :, cut])
             state = 0.5 * twice_gelu(value + skip_col[...])
             halves = state.reshape(C, 2, 8, 256)
             for h in range(2):
@@ -446,11 +494,26 @@
     v = pltpu.VMEM
     dma = pltpu.SemaphoreType.DMA
     buffers = [
-        v((R, 32, LW), bf16),
-        v((R, 32, LW), bf16),
+        v((2, 320, 1024), bf16),
+        v((9, PK, W2), bf16),
+        v((1024, 384), bf16),
+        v((384, 1024), bf16),
+        v((48, 128), bf16),
+        v((256, 24), bf16),
+        v((R, 48, 16), bf16),
+        v((R, 32, 24), bf16),
+        v((LW, 128), bf16),
+        v((128, LW), bf16),
+        v((128, LW), bf16),
+        v((128, LW), bf16),
+        v((LW, 128), bf16),
+        v((LW, 128), bf16),
+        v((256, 256), bf16),
+        v((R, 2, 16, LW), bf16),
+        v((2, R, 16, LW), bf16),
         v((384, 128), f32),
-        v((R, 48, 128), bf16),
-        v((R, 48, 128), bf16),
+        v((R, 2, 24, 128), bf16),
+        v((R, 2, 24, 128), bf16),
         v((384, 128), f32),
         v((576, 128), f32),
         v((R, 80, 128), bf16),
@@ -466,12 +529,12 @@
         v((R, 80, 128), bf16),
         v((576, 128), f32),
         v((384, 128), f32),
-        v((R, 48, 128), bf16),
-        v((R, 48, 128), bf16),
+        v((R, 2, 24, 128), bf16),
+        v((R, 2, 24, 128), bf16),
         v((384, 128), f32),
-        v((R, 32, LW), bf16),
-        v((R, 32, LW), bf16),
-        v((640, 384), bf16),
+        v((R, 2, 16, LW), bf16),
+        v((2, R, 16, LW), bf16),
+        v((320, 384), bf16),
         v((32, 1024), f32),
         v((256, 128), f32),
         v((R, 32, 128), bf16),
@@ -489,9 +552,10 @@
         v((512, 256), f32),
         v((512, 256), f32),
     ]
-    sems = []
-    for count in (7, 7, 7, 7, 7, 7, 3, 3, 3, 3, 3, 3, 7, 7, 7, 7, 7, 7, 7, 7, 7, 7):
-        sems.append(dma((count,)))
+    pairs_of = lambda count: [dma((count,)), dma((count,))]
+    by_x = [dma((2, 7)), dma((2, 7))]
+    sems = [dma((16,))] + by_x + by_x + pairs_of(7)
+    sems += [dma((3,))] * 6 + pairs_of(7) + by_x + by_x + pairs_of(7) + pairs_of(7)
     return buffers + sems
 
 
@@ -509,7 +573,7 @@
 ):
     tables = [jnp.asarray(t) for t in constants()]
     args = [
-        jnp.transpose(field, (0, 2, 1, 3)).reshape(640, Z * T_SIZE),
+        jnp.transpose(field, (0, 2, 1, 3)).reshape(2, 320, Z * T_SIZE),
         spectral_weight,
         skip_weight,
         skip_bias.reshape(1, C),
@@ -521,10 +585,11 @@
         recv_rows.reshape(1, 100),
     ] + tables
     vmem = pl.BlockSpec(memory_space=pltpu.VMEM)
+    hbm = pl.BlockSpec(memory_space=pl.ANY)
     result = pl.pallas_call(
         kernel,
         out_shape=jax.ShapeDtypeStruct((100, 128), bf16),
-        in_specs=[vmem] * len(args),
+        in_specs=[hbm] * 2 + [vmem] * 8 + [hbm] * len(tables),
         out_specs=vmem,
         scratch_shapes=scratch(),
         compiler_params=pltpu.CompilerParams(

time: 97.5 us -> 94.7 us (0.971)
  Pallas kernels: 95.7 us -> 93.1 us
    pallas_call x1, Pallas kernels: 95.7 us -> 93.1 us  [local(): pl.pallas_call(kernel, out_shape=jax.ShapeDtypeStruct((100, 128), bf16),...]
where the time goes in v2:
time: 94.7 us; the launch traced here: 94.5 us
  Pallas kernels  93.1 us (98%)
  local copies, waits for them, and re-layouts  1.35 us (1%)
    pallas_call x1, Pallas kernels, local(): pl.pallas_call(kernel, out_shape=jax.ShapeDtypeStruct((100, 128), bf16),...  93.1 us

profile of v2, /device:TPU:1, one launch (start us, length us, event | category | flops | bytes accessed | tf_op | source)
XLA Modules:
  0.0 94.5 jit_solution(10155758169962037046)
XLA Ops:
  0.0 93.1 %shard_map.217 = bf16[100,128]{1,0:T(8,128)(2,1)} custom-call(bf16[2,320,1024]{2,1,0:T(8,128)(2,1)} %bitcast.10, bf16[9,18,800]{2,1,0:T(8,128)(2,1)} %refs_1_.1, bf16[20,20]{1,0:T(8,128)(2,1)} %refs_2_.1, f32[1,20]{1,0:T(1,128)} %bitcast.14, bf16[20,64]{1,0:T(8,128)(2,1)} %refs_4_.1, f32[1,64]{1,0:T(1,128)} %bitcast.15, bf16[1,64]{1,0:T(2,128)(2,1)} %bitcast.16, ...), custom_call_target="tpu_custom_call" | custom-call | tf_op jit(solution)/shard_map/pallas_call | solution.py:589
  93.1 1.4 %copy.25 = bf16[1,1,100,128]{3,2,1,0:T(8,128)(2,1)} copy(bf16[1,1,100,128]{3,2,1,0:T(8,128)(2,1)} %bitcast.11) | data formatting | bytes 51200

commit v3 on v2

--- a/solution.py
+++ b/solution.py
@@ -121,12 +121,12 @@
         out,
         field, weight, t_fwd, t_bwd, y_fwd, y_bwd, x_fwd, x_bwd, gather, spread,
         widen, widen_sw, sum_re, sum_im, regroup,
-        send_y, recv_y, ya, send_a, recv_a, xa, xb, send_b, recv_b, spec_b, spec_p,
-        pairs, amat, mix, mix_p, mix_b, send_c, recv_c, xc, xd, send_d, recv_d, xe, send_e, recv_e,
+        send_y, recv_y, ya, send_a, recv_a, xa, xb, send_b, recv_b,
+        pairs, amat, mix, send_c, recv_c, xc, xd, send_d, recv_d, xe, send_e, recv_e,
         s6, part, blk, send_f, recv_f, send_g, recv_g, wpad, perm, pick, idrows, square, skip_k, hid_k,
         skip_col, hid_col, out_col,
         fetched,
-        ss_y, rs_y, ss_a, rs_a, ss_b, rs_b, ss_p, rs_p, ls_p, ss_q, rs_q, ls_q, ss_c, rs_c,
+        ss_y, rs_y, ss_a, rs_a, ss_b, rs_b, ss_p, rs_p, ls_p, ss_c, rs_c,
         ss_d, rs_d, ss_e, rs_e, ss_f, rs_f, ss_g, rs_g,
     ) = refs
     i = lax.axis_index("gx")
@@ -169,7 +169,7 @@
     fetch = []
     wanted = [
         (field_in.at[0], field.at[0]), (t_fwd_in, t_fwd), (field_in.at[1], field.at[1]),
-        (y_fwd_in, y_fwd), (weight_in, weight), (x_fwd_in, x_fwd), (gather_in, gather),
+        (y_fwd_in, y_fwd), (x_fwd_in, x_fwd), (gather_in, gather),
         (widen_in, widen), (widen_sw_in, widen_sw), (sum_re_in, sum_re), (sum_im_in, sum_im),
         (spread_in, spread), (x_bwd_in, x_bwd), (y_bwd_in, y_bwd), (t_bwd_in, t_bwd),
         (regroup_in, regroup),
@@ -178,48 +178,96 @@
         fetch.append(pltpu.make_async_copy(source, target, fetched.at[n]))
         fetch[n].start()
 
-    def exchange_copies(near, me, send, recv, send_sem, recv_sem, same=False):
-        copies = []
+    sent = []
+
+    def await_bytes(view, sem):
+        pltpu.make_async_copy(view, view, sem).wait()
+
+    def start(near, me, send, recv, send_sem, recv_sem):
         for d in range(1, R):
             peer, device = near(d)
-            copies.append(
-                pltpu.make_async_remote_copy(
-                    src_ref=send if same else send(peer),
-                    dst_ref=recv(me),
-                    send_sem=send_sem.at[d - 1],
-                    recv_sem=recv_sem.at[d - 1],
-                    device_id=device,
-                    device_id_type=MESH,
-                )
-            )
-        return copies
-
-    def start(copies):
-        for copy in copies:
-            copy.start()
-
-    def finish(copies):
-        for copy in copies:
-            copy.wait()
+            pltpu.make_async_remote_copy(
+                src_ref=send(peer),
+                dst_ref=recv(me),
+                send_sem=send_sem,
+                recv_sem=recv_sem,
+                device_id=device,
+                device_id_type=MESH,
+            ).start()
 
     def exchange(near, me, send, recv, send_sem, recv_sem, same=False):
-        copies = exchange_copies(
-            near, me, send if same else lambda p: send.at[p], lambda p: recv.at[p],
-            send_sem, recv_sem, same,
+        start(
+            near, me, (lambda p: send) if same else (lambda p: send.at[p]), lambda p: recv.at[p],
+            send_sem.at[0], recv_sem.at[0],
         )
-        start(copies)
         recv[me] = send[...] if same else send[me]
-        finish(copies)
-
-    def copies_y(x, send, recv, send_sem, recv_sem):
-        return exchange_copies(
+        seven = recv.at[pl.ds(0, R - 1)]
+        sent.append((seven, send_sem.at[0]))
+        await_bytes(seven, recv_sem.at[0])
+
+    def start_y(x, send, recv, send_sem, recv_sem):
+        start(
             on_y, j, lambda p: send.at[p, x], lambda p: recv.at[x, p], send_sem.at[x], recv_sem.at[x]
         )
-
-    def copies_z(x, send, recv, send_sem, recv_sem):
-        return exchange_copies(
-            on_z, zh, lambda p: send.at[p, x], lambda p: recv.at[p, x], send_sem.at[x], recv_sem.at[x]
+        recv[x, j] = send[j, x]
+        sent.append((recv.at[x, pl.ds(0, R - 1)], send_sem.at[x]))
+
+    def finish_y(x, recv, recv_sem):
+        await_bytes(recv.at[x, pl.ds(0, R - 1)], recv_sem.at[x])
+
+    def start_z(x, send, recv, send_sem, recv_sem):
+        start(
+            on_z, zh, lambda p: send.at[p, x], lambda p: recv.at[x, p], send_sem.at[x], recv_sem.at[x]
         )
+        recv[x, zh] = send[zh, x]
+        sent.append((recv.at[x, pl.ds(0, R - 1)], send_sem.at[x]))
+
+    def weights_copy(n, a, device):
+        return pltpu.make_async_remote_copy(
+            src_ref=weight_in.at[n],
+            dst_ref=weight.at[a],
+            send_sem=ss_p.at[n],
+            recv_sem=rs_p.at[a],
+            device_id=(device, j),
+            device_id_type=MESH,
+        )
+
+    def weights_kept(n, a):
+        return pltpu.make_async_copy(weight_in.at[n], weight.at[a], ls_p.at[n])
+
+    def start_weights():
+        for n, (device, a) in enumerate(sources):
+
+            @pl.when(device != i)
+            def _():
+                weights_copy(n, a, device).start()
+
+            @pl.when(device == i)
+            def _():
+                weights_kept(n, a).start()
+
+    def finish_weights():
+        for n, (device, a) in enumerate(sources):
+
+            @pl.when(device == i)
+            def _():
+                weights_kept(n, a).wait()
+
+        for a, (device, n) in enumerate(owners):
+
+            @pl.when(device != i)
+            def _():
+                weights_copy(n, a, device).wait_recv()
+
+    def finish_sends():
+        for n, (device, a) in enumerate(sources):
+
+            @pl.when(device != i)
+            def _():
+                weights_copy(n, a, device).wait_send()
+
+        for view, sem in sent:
+            await_bytes(view, sem)
 
     lane = iota((1, 128), 1)
     in_half = lane & 63
@@ -263,20 +311,16 @@
         expected = expected + jnp.where(other != i, 1, 0)
     pl.semaphore_wait(barrier, expected)
 
-    going_y = [copies_y(x, send_y, recv_y, ss_y, rs_y) for x in range(2)]
-    start(going_y[0])
+    start_y(0, send_y, recv_y, ss_y, rs_y)
+    start_weights()
     fetch[2].wait()
     along_zt(1)
-    start(going_y[1])
-    for x in range(2):
-        recv_y[x, j] = send_y[j, x]
+    start_y(1, send_y, recv_y, ss_y, rs_y)
     for copy in fetch[3:]:
         copy.wait()
 
     def prepare():
         wpad[...] = jnp.zeros((288, LW), bf16)
-        for p in range(9):
-            wpad[32 * p : 32 * p + PK, 0:W2] = weight[p]
         ya[...] = jnp.zeros((384, 128), f32)
         xb[...] = jnp.zeros((576, 128), f32)
         xd[...] = jnp.zeros((384, 128), f32)
@@ -321,9 +365,8 @@
 
     prepare()
 
-    going_a = [copies_z(x, send_a, recv_a, ss_a, rs_a) for x in range(2)]
     for x in range(2):
-        finish(going_y[x])
+        finish_y(x, recv_y, rs_y)
         got = mm(y_fwd[...], recv_y[x].reshape(Y, LW))
         for g in range(G):
             part_g = got[:, 128 * g : 128 * g + 128]
@@ -331,13 +374,13 @@
                 part_g[0:MY], part_g[MY : 2 * MY], fwd_sign
             )
         send_a[:, x] = ya[192 * x : 192 * x + 192, :].astype(bf16).reshape(R, 24, 128)
-        start(going_a[x])
-        recv_a[zh, x] = send_a[zh, x]
-    finish(going_a[0])
-    finish(going_a[1])
+        start_z(x, send_a, recv_a, ss_a, rs_a)
+    for x in range(2):
+        finish_y(x, recv_a, rs_a)
 
     for p in range(R):
-        xa[48 * p : 48 * p + 48, :] = recv_a[p].astype(f32).reshape(48, 128)
+        for x in range(2):
+            xa[48 * p + 24 * x : 48 * p + 24 * x + 24, :] = recv_a[x, p].astype(f32)
     used = [8 * a + g for a in range(3) for g in range(G)]
     data = jnp.concatenate(
         [xa[pl.ds(u, 16, stride=24), :] for u in used], axis=1
@@ -347,59 +390,20 @@
         part_u = got[:, 128 * n : 128 * n + 128]
         xb[pl.ds(u, MX, stride=24), :] = combine(part_u[0:MX], part_u[MX : 2 * MX], fwd_sign)
     for p in range(R):
-        send_b[p] = jnp.concatenate(
-            [xb[72 * p : 72 * p + 72, :], jnp.zeros((8, 128), f32)], axis=0
-        ).astype(bf16)
+        send_b[p] = xb[72 * p : 72 * p + 72, :].astype(bf16)
     exchange(on_e, e, send_b, recv_b, ss_b, rs_b)
     total = recv_b[0].astype(f32)
     for p in range(1, R):
         total = total + recv_b[p].astype(f32)
-    for n in range(3):
-        spec_b[n] = total[24 * n : 24 * n + 24]
-
-    def own_copy(src, n, dst, a, send_sem, recv_sem, device):
-        return pltpu.make_async_remote_copy(
-            src_ref=src.at[n],
-            dst_ref=dst.at[a],
-            send_sem=send_sem.at[n],
-            recv_sem=recv_sem.at[a],
-            device_id=(device, j),
-            device_id_type=MESH,
-        )
-
-    def hand_over(src, dst, targets, origins, send_sem, recv_sem, local_sem):
-        for n, (device, a) in enumerate(targets):
-
-            @pl.when(device != i)
-            def _():
-                own_copy(src, n, dst, a, send_sem, recv_sem, device).start()
-
-            @pl.when(device == i)
-            def _():
-                copy = pltpu.make_async_copy(src.at[n], dst.at[a], local_sem.at[n])
-                copy.start()
-                copy.wait()
-
-        for n, (device, a) in enumerate(targets):
-
-            @pl.when(device != i)
-            def _():
-                own_copy(src, n, dst, a, send_sem, recv_sem, device).wait_send()
-
-        for a, (device, n) in enumerate(origins):
-
-            @pl.when(device != i)
-            def _():
-                own_copy(src, n, dst, a, send_sem, recv_sem, device).wait_recv()
-
-    hand_over(spec_b, spec_p, owners, sources, ss_p, rs_p, ls_p)
+    pairs[...] = total
+    finish_weights()
+    for p in range(9):
+        wpad[32 * p : 32 * p + PK, 0:W2] = weight[p // 3, p % 3]
 
     own_k = one_hot(
         (iota((32, 128), 1) & 63 < 3 * PK)
         & (lax.rem(iota((32, 128), 1) & 63, PK) == iota((32, 128), 0))
     )
-    for n in range(3):
-        pairs[24 * n : 24 * n + 24, :] = spec_p[n]
     for p in range(9):
         for g in range(G):
             row = jnp.broadcast_to(pairs[8 * p + g : 8 * p + g + 1, :], (32, 128))
@@ -414,17 +418,11 @@
         for g in range(G):
             tile = wide[32 * p : 32 * p + 32, 128 * g : 128 * g + 128] * own_k
             mix[8 * p + g : 8 * p + g + 1, :] = jnp.sum(tile, axis=0, keepdims=True)
-    for a in range(3):
-        mix_p[a] = mix[24 * a : 24 * a + 24, :]
-
-    hand_over(mix_p, mix_b, sources, owners, ss_q, rs_q, ls_q)
-    send_c[...] = jnp.concatenate(
-        [mix_b[0], mix_b[1], mix_b[2], jnp.zeros((8, 128), f32)], axis=0
-    ).astype(bf16)
+    send_c[...] = mix[...].astype(bf16)
     exchange(on_e, e, send_c, recv_c, ss_c, rs_c, same=True)
 
     for p in range(R):
-        xc[72 * p : 72 * p + 72, :] = recv_c[p].astype(f32)[0:72]
+        xc[72 * p : 72 * p + 72, :] = recv_c[p].astype(f32)
     data = jnp.concatenate(
         [xc[pl.ds(u, MX, stride=24), :] for u in used], axis=1
     ).astype(bf16)
@@ -432,18 +430,15 @@
     for n, u in enumerate(used):
         part_u = got[:, 128 * n : 128 * n + 128]
         xd[pl.ds(u, 16, stride=24), :] = combine(part_u[0:16], part_u[16:32], -fwd_sign)
-    going_d = [copies_z(x, send_d, recv_d, ss_d, rs_d) for x in range(2)]
     for x in range(2):
         for p in range(R):
             send_d[p, x] = xd[48 * p + 24 * x : 48 * p + 24 * x + 24, :].astype(bf16)
-        start(going_d[x])
-        recv_d[zh, x] = send_d[zh, x]
-
-    going_e = [copies_y(x, send_e, recv_e, ss_e, rs_e) for x in range(2)]
+        start_z(x, send_d, recv_d, ss_d, rs_d)
+
     for x in range(2):
-        finish(going_d[x])
+        finish_y(x, recv_d, rs_d)
         for p in range(R):
-            xe[192 * x + 24 * p : 192 * x + 24 * p + 24, :] = recv_d[p, x].astype(f32)
+            xe[192 * x + 24 * p : 192 * x + 24 * p + 24, :] = recv_d[x, p].astype(f32)
         data = jnp.concatenate(
             [xe[pl.ds(192 * x + g, MY, stride=8), :] for g in range(G)], axis=1
         ).astype(bf16)
@@ -452,12 +447,11 @@
             part_g = got[:, 128 * g : 128 * g + 128]
             turned = combine(part_g[0:Y], part_g[Y : 2 * Y], -fwd_sign).astype(bf16)
             send_e[:, x, :, 128 * g : 128 * g + 128] = turned.reshape(R, 16, 128)
-        start(going_e[x])
-        recv_e[x, j] = send_e[j, x]
+        start_y(x, send_e, recv_e, ss_e, rs_e)
 
     @pl.loop(0, 2)
     def _(x):
-        finish(copies_y(x, send_e, recv_e, ss_e, rs_e))
+        finish_y(x, recv_e, rs_e)
         for t in range(3):
             for g in range(G):
                 held = [
@@ -488,6 +482,7 @@
     exchange(on_e, e, send_g, recv_g, ss_g, rs_g)
     owned = mm(pick[...], recv_g[...].reshape(256, 128))
     out[...] = owned[0:100].astype(bf16)
+    finish_sends()
 
 
 def scratch():
@@ -495,7 +490,7 @@
     dma = pltpu.SemaphoreType.DMA
     buffers = [
         v((2, 320, 1024), bf16),
-        v((9, PK, W2), bf16),
+        v((3, 3, PK, W2), bf16),
         v((1024, 384), bf16),
         v((384, 1024), bf16),
         v((48, 128), bf16),
@@ -513,24 +508,20 @@
         v((2, R, 16, LW), bf16),
         v((384, 128), f32),
         v((R, 2, 24, 128), bf16),
-        v((R, 2, 24, 128), bf16),
+        v((2, R, 24, 128), bf16),
         v((384, 128), f32),
         v((576, 128), f32),
-        v((R, 80, 128), bf16),
-        v((R, 80, 128), bf16),
-        v((3, 24, 128), f32),
-        v((3, 24, 128), f32),
+        v((R, 72, 128), bf16),
+        v((R, 72, 128), bf16),
         v((72, 128), f32),
         v((288, LW), bf16),
         v((72, 128), f32),
-        v((3, 24, 128), f32),
-        v((3, 24, 128), f32),
-        v((80, 128), bf16),
-        v((R, 80, 128), bf16),
+        v((72, 128), bf16),
+        v((R, 72, 128), bf16),
         v((576, 128), f32),
         v((384, 128), f32),
         v((R, 2, 24, 128), bf16),
-        v((R, 2, 24, 128), bf16),
+        v((2, R, 24, 128), bf16),
         v((384, 128), f32),
         v((R, 2, 16, LW), bf16),
         v((2, R, 16, LW), bf16),
@@ -552,10 +543,8 @@
         v((512, 256), f32),
         v((512, 256), f32),
     ]
-    pairs_of = lambda count: [dma((count,)), dma((count,))]
-    by_x = [dma((2, 7)), dma((2, 7))]
-    sems = [dma((16,))] + by_x + by_x + pairs_of(7)
-    sems += [dma((3,))] * 6 + pairs_of(7) + by_x + by_x + pairs_of(7) + pairs_of(7)
+    one, by_x = [dma((1,))] * 2, [dma((2,))] * 2
+    sems = [dma((15,))] + by_x + by_x + one + [dma((3,))] * 3 + one + by_x + by_x + one + one
     return buffers + sems
 
 
@@ -574,7 +563,7 @@
     tables = [jnp.asarray(t) for t in constants()]
     args = [
         jnp.transpose(field, (0, 2, 1, 3)).reshape(2, 320, Z * T_SIZE),
-        spectral_weight,
+        spectral_weight.reshape(3, 3, PK, W2),
         skip_weight,
         skip_bias.reshape(1, C),
         hidden_weight,

time: 94.7 us -> 94.1 us (level)
  no operation moved by 1% of the time
where the time goes in v3:
time: 94.1 us; the launch traced here: 93.9 us
  Pallas kernels  92.5 us (98%)
  local copies, waits for them, and re-layouts  1.35 us (1%)
    pallas_call x1, Pallas kernels, local(): pl.pallas_call(kernel, out_shape=jax.ShapeDtypeStruct((100, 128), bf16),...  92.5 us

profile of v3, /device:TPU:1, one launch (start us, length us, event | category | flops | bytes accessed | tf_op | source)
XLA Modules:
  0.0 93.9 jit_solution(17885745244566212186)
XLA Ops:
  0.0 92.5 %shard_map.217 = bf16[100,128]{1,0:T(8,128)(2,1)} custom-call(bf16[2,320,1024]{2,1,0:T(8,128)(2,1)} %bitcast.11, bf16[3,3,18,800]{3,2,1,0:T(8,128)(2,1)} %bitcast.12, bf16[20,20]{1,0:T(8,128)(2,1)} %refs_2_.1, f32[1,20]{1,0:T(1,128)} %bitcast.16, bf16[20,64]{1,0:T(8,128)(2,1)} %refs_4_.1, f32[1,64]{1,0:T(1,128)} %bitcast.17, bf16[1,64]{1,0:T(2,128)(2,1)} %bitcast.18, ...), custom_call_target="tpu_custom_call" | custom-call | tf_op jit(solution)/shard_map/pallas_call | solution.py:578
  92.5 1.4 %copy.25 = bf16[1,1,100,128]{3,2,1,0:T(8,128)(2,1)} copy(bf16[1,1,100,128]{3,2,1,0:T(8,128)(2,1)} %bitcast.13) | data formatting | bytes 51200

commit v4 on v3

--- a/solution.py
+++ b/solution.py
@@ -123,7 +123,7 @@
         widen, widen_sw, sum_re, sum_im, regroup,
         send_y, recv_y, ya, send_a, recv_a, xa, xb, send_b, recv_b,
         pairs, amat, mix, send_c, recv_c, xc, xd, send_d, recv_d, xe, send_e, recv_e,
-        s6, part, blk, send_f, recv_f, send_g, recv_g, wpad, perm, pick, idrows, square, skip_k, hid_k,
+        s6, s1, wide, part, blk, send_f, recv_f, send_g, recv_g, wpad, perm, pick, idrows, square, skip_k, hid_k,
         skip_col, hid_col, out_col,
         fetched,
         ss_y, rs_y, ss_a, rs_a, ss_b, rs_b, ss_p, rs_p, ls_p, ss_c, rs_c,
@@ -168,7 +168,7 @@
 
     fetch = []
     wanted = [
-        (field_in.at[0], field.at[0]), (t_fwd_in, t_fwd), (field_in.at[1], field.at[1]),
+        (t_fwd_in, t_fwd), (field_in.at[0], field.at[0]), (field_in.at[1], field.at[1]),
         (y_fwd_in, y_fwd), (x_fwd_in, x_fwd), (gather_in, gather),
         (widen_in, widen), (widen_sw_in, widen_sw), (sum_re_in, sum_re), (sum_im_in, sum_im),
         (spread_in, spread), (x_bwd_in, x_bwd), (y_bwd_in, y_bwd), (t_bwd_in, t_bwd),
@@ -195,7 +195,7 @@
                 device_id_type=MESH,
             ).start()
 
-    def exchange(near, me, send, recv, send_sem, recv_sem, same=False):
+    def exchange(near, me, send, recv, send_sem, recv_sem, same=False, beside=None):
         start(
             near, me, (lambda p: send) if same else (lambda p: send.at[p]), lambda p: recv.at[p],
             send_sem.at[0], recv_sem.at[0],
@@ -203,6 +203,8 @@
         recv[me] = send[...] if same else send[me]
         seven = recv.at[pl.ds(0, R - 1)]
         sent.append((seven, send_sem.at[0]))
+        if beside is not None:
+            beside()
         await_bytes(seven, recv_sem.at[0])
 
     def start_y(x, send, recv, send_sem, recv_sem):
@@ -210,7 +212,6 @@
             on_y, j, lambda p: send.at[p, x], lambda p: recv.at[x, p], send_sem.at[x], recv_sem.at[x]
         )
         recv[x, j] = send[j, x]
-        sent.append((recv.at[x, pl.ds(0, R - 1)], send_sem.at[x]))
 
     def finish_y(x, recv, recv_sem):
         await_bytes(recv.at[x, pl.ds(0, R - 1)], recv_sem.at[x])
@@ -220,7 +221,6 @@
             on_z, zh, lambda p: send.at[p, x], lambda p: recv.at[x, p], send_sem.at[x], recv_sem.at[x]
         )
         recv[x, zh] = send[zh, x]
-        sent.append((recv.at[x, pl.ds(0, R - 1)], send_sem.at[x]))
 
     def weights_copy(n, a, device):
         return pltpu.make_async_remote_copy(
@@ -268,6 +268,9 @@
 
         for view, sem in sent:
             await_bytes(view, sem)
+        for recv, send_sem in ((recv_y, ss_y), (recv_a, ss_a), (recv_d, ss_d), (recv_e, ss_e)):
+            for x in range(2):
+                await_bytes(recv.at[x, pl.ds(0, R - 1)], send_sem.at[x])
 
     lane = iota((1, 128), 1)
     in_half = lane & 63
@@ -289,42 +292,62 @@
     def combine(cosines, sines, sign):
         return cosines + sign * pltpu.roll(sines, 64, 1)
 
-    def along_zt(x):
-        got = mm(field[x], t_fwd[...])
-        for g in range(G):
-            for t in range(3):
-                held = [
-                    got[16 * c : 16 * c + 16, 128 * t : 128 * t + 128] if c < C else None
-                    for c in range(3 * g, 3 * g + 3)
-                ]
-                for n in range(min(3, R - 3 * t)):
-                    send_y[3 * t + n, x, :, 128 * g : 128 * g + 128] = (
-                        regrouped(held, n).astype(bf16)
-                    )
-
-    fetch[0].wait()
-    fetch[1].wait()
-    along_zt(0)
-
     expected = 3 * (R - 1)
     for other, _ in owners + sources:
         expected = expected + jnp.where(other != i, 1, 0)
-    pl.semaphore_wait(barrier, expected)
-
-    start_y(0, send_y, recv_y, ss_y, rs_y)
-    start_weights()
-    fetch[2].wait()
-    along_zt(1)
-    start_y(1, send_y, recv_y, ss_y, rs_y)
+
+    s1[320:336, :] = jnp.zeros((16, 384), f32)
+    fetch[0].wait()
+
+    @pl.loop(0, 2)
+    def _(x):
+        pltpu.make_async_copy(field_in.at[x], field.at[x], fetched.at[1 + x]).wait()
+        s1[0:320, :] = mm(field[x], t_fwd[...])
+
+        @pl.loop(0, G)
+        def _(g):
+            lanes = pl.ds(pl.multiple_of(128 * g, 128), 128)
+            for t in range(3):
+                held = [
+                    s1[pl.ds(pl.multiple_of(48 * g + 16 * m, 16), 16), 128 * t : 128 * t + 128]
+                    for m in range(3)
+                ]
+                for n in range(min(3, R - 3 * t)):
+                    send_y[3 * t + n, x, :, lanes] = regrouped(held, n).astype(bf16)
+
+        @pl.when(x == 0)
+        def _():
+            pl.semaphore_wait(barrier, expected)
+
+        start_y(x, send_y, recv_y, ss_y, rs_y)
+
+        @pl.when(x == 0)
+        def _():
+            start_weights()
+
     for copy in fetch[3:]:
         copy.wait()
 
-    def prepare():
+    def spread_map(values, rows, cols, places):
+        shift = places.bit_length() - 1
+        left = one_hot((iota((rows, 128), 0) >> shift) == iota((rows, 128), 1)).astype(bf16)
+        right = one_hot((iota((128, cols), 1) >> shift) == iota((128, cols), 0)).astype(bf16)
+        wide = mm(mm(left, values.T.astype(bf16)).astype(bf16), right)
+        same = (iota((rows, cols), 0) & (places - 1)) == (iota((rows, cols), 1) & (places - 1))
+        return jnp.where(same, wide, 0.0).astype(bf16)
+
+    def column(values, places, width, rows):
+        shift = places.bit_length() - 1
+        at = one_hot((iota((rows, width), 0) >> shift) == iota((rows, width), 1))
+        return jnp.broadcast_to(jnp.sum(at * values, axis=1, keepdims=True), (rows, 128))
+
+    def prepare_clear():
         wpad[...] = jnp.zeros((288, LW), bf16)
-        ya[...] = jnp.zeros((384, 128), f32)
+        ya[...] = jnp.zeros((192, 128), f32)
         xb[...] = jnp.zeros((576, 128), f32)
         xd[...] = jnp.zeros((384, 128), f32)
-        mix[...] = jnp.zeros((72, 128), f32)
+
+    def prepare_rows():
         idrows[...] = jnp.full((8, 256), -1, jnp.int32)
         idrows[0:1, 0:200] = b_ids[...]
         idrows[1:2, 0:200] = s_rows[...]
@@ -338,43 +361,38 @@
         place = iota((256, 128), 0)
         name = ((place >> 2) & 7) * 32 + (place >> 5) * 4 + (place & 3)
         pick[...] = one_hot(name == idrows[2:3, 0:128]).T.astype(bf16)
-        def spread_map(values, rows, cols, places):
-            shift = places.bit_length() - 1
-            left = one_hot((iota((rows, 128), 0) >> shift) == iota((rows, 128), 1)).astype(bf16)
-            right = one_hot((iota((128, cols), 1) >> shift) == iota((128, cols), 0)).astype(bf16)
-            wide = mm(mm(left, values.T.astype(bf16)).astype(bf16), right)
-            same = (iota((rows, cols), 0) & (places - 1)) == (iota((rows, cols), 1) & (places - 1))
-            return jnp.where(same, wide, 0.0).astype(bf16)
-
+
+    def prepare_skip():
         square[...] = jnp.zeros((128, 128), f32)
         square[0:C, 0:C] = skip_w[...].astype(f32)
         skip_k[...] = spread_map(square[...], 320, 320, 16)
+        skip_col[...] = column(skip_b[...], 16, C, 320)
+
+    def prepare_hidden():
+        square[...] = jnp.zeros((128, 128), f32)
         square[0:C, 0:HID] = hid_w[...].astype(f32)
         hid_k[...] = spread_map(square[...], 512, 160, 8)
-
-        def column(values, places, width, rows):
-            shift = places.bit_length() - 1
-            at = one_hot((iota((rows, width), 0) >> shift) == iota((rows, width), 1))
-            return jnp.broadcast_to(
-                jnp.sum(at * values, axis=1, keepdims=True), (rows, 256)
-            )
-
-        skip_col[...] = column(skip_b[...], 16, C, 320)
         hid_col[...] = column(hid_b[...], 8, HID, 512)
+
+    def prepare_out():
         out_col[...] = column(0.5 * out_w[...].astype(f32), 8, HID, 512)
 
-    prepare()
-
-    for x in range(2):
+    prepare_clear()
+    prepare_skip()
+
+    @pl.loop(0, 2)
+    def _(x):
         finish_y(x, recv_y, rs_y)
         got = mm(y_fwd[...], recv_y[x].reshape(Y, LW))
         for g in range(G):
             part_g = got[:, 128 * g : 128 * g + 128]
-            ya[pl.ds(192 * x + g, MY, stride=8), :] = combine(
+            ya[pl.ds(g, MY, stride=8), :] = combine(
                 part_g[0:MY], part_g[MY : 2 * MY], fwd_sign
             )
-        send_a[:, x] = ya[192 * x : 192 * x + 192, :].astype(bf16).reshape(R, 24, 128)
+        send_a[:, x] = ya[...].astype(bf16).reshape(R, 24, 128)
         start_z(x, send_a, recv_a, ss_a, rs_a)
+
+    prepare_hidden()
     for x in range(2):
         finish_y(x, recv_a, rs_a)
 
@@ -391,7 +409,7 @@
         xb[pl.ds(u, MX, stride=24), :] = combine(part_u[0:MX], part_u[MX : 2 * MX], fwd_sign)
     for p in range(R):
         send_b[p] = xb[72 * p : 72 * p + 72, :].astype(bf16)
-    exchange(on_e, e, send_b, recv_b, ss_b, rs_b)
+    exchange(on_e, e, send_b, recv_b, ss_b, rs_b, beside=prepare_out)
     total = recv_b[0].astype(f32)
     for p in range(1, R):
         total = total + recv_b[p].astype(f32)
@@ -404,22 +422,35 @@
         (iota((32, 128), 1) & 63 < 3 * PK)
         & (lax.rem(iota((32, 128), 1) & 63, PK) == iota((32, 128), 0))
     )
-    for p in range(9):
+
+    @pl.loop(0, 9)
+    def _(p):
+        rows = pl.ds(pl.multiple_of(32 * p, 32), 32)
+        eight = pairs[pl.ds(pl.multiple_of(8 * p, 8), 8), :]
         for g in range(G):
-            row = jnp.broadcast_to(pairs[8 * p + g : 8 * p + g + 1, :], (32, 128))
-            amat[32 * p : 32 * p + 32, 128 * g : 128 * g + 128] = (row * own_k).astype(bf16)
+            row = jnp.broadcast_to(eight[g : g + 1, :], (32, 128))
+            amat[rows, 128 * g : 128 * g + 128] = (row * own_k).astype(bf16)
+
     compact = mm(amat[...], gather[...]).astype(bf16)
     weights = wpad[...].astype(f32)
     straight = (mm(compact, widen[...]) * weights).astype(bf16)
     crossed = (mm(compact, widen_sw[...]) * weights).astype(bf16)
     mixed = (mm(straight, sum_re[...]) + mm(crossed, sum_im[...])).astype(bf16)
-    wide = mm(mixed, spread[...])
-    for p in range(9):
-        for g in range(G):
-            tile = wide[32 * p : 32 * p + 32, 128 * g : 128 * g + 128] * own_k
-            mix[8 * p + g : 8 * p + g + 1, :] = jnp.sum(tile, axis=0, keepdims=True)
+    wide[...] = mm(mixed, spread[...])
+
+    @pl.loop(0, 9)
+    def _(p):
+        rows = pl.ds(pl.multiple_of(32 * p, 32), 32)
+        sums = [
+            jnp.sum(wide[rows, 128 * g : 128 * g + 128] * own_k, axis=0, keepdims=True)
+            for g in range(G)
+        ]
+        mix[pl.ds(pl.multiple_of(8 * p, 8), 8), :] = jnp.concatenate(
+            sums + [jnp.zeros((1, 128), f32)], axis=0
+        )
+
     send_c[...] = mix[...].astype(bf16)
-    exchange(on_e, e, send_c, recv_c, ss_c, rs_c, same=True)
+    exchange(on_e, e, send_c, recv_c, ss_c, rs_c, same=True, beside=prepare_rows)
 
     for p in range(R):
         xc[72 * p : 72 * p + 72, :] = recv_c[p].astype(f32)
@@ -435,12 +466,12 @@
             send_d[p, x] = xd[48 * p + 24 * x : 48 * p + 24 * x + 24, :].astype(bf16)
         start_z(x, send_d, recv_d, ss_d, rs_d)
 
-    for x in range(2):
+    @pl.loop(0, 2)
+    def _(x):
         finish_y(x, recv_d, rs_d)
-        for p in range(R):
-            xe[192 * x + 24 * p : 192 * x + 24 * p + 24, :] = recv_d[x, p].astype(f32)
+        xe[...] = recv_d[x].astype(f32).reshape(192, 128)
         data = jnp.concatenate(
-            [xe[pl.ds(192 * x + g, MY, stride=8), :] for g in range(G)], axis=1
+            [xe[pl.ds(g, MY, stride=8), :] for g in range(G)], axis=1
         ).astype(bf16)
         got = mm(y_bwd[...], data)
         for g in range(G):
@@ -452,23 +483,32 @@
     @pl.loop(0, 2)
     def _(x):
         finish_y(x, recv_e, rs_e)
-        for t in range(3):
-            for g in range(G):
+
+        @pl.loop(0, G)
+        def _(g):
+            lanes = pl.ds(pl.multiple_of(128 * g, 128), 128)
+            for t in range(3):
                 held = [
-                    recv_e[x, n, :, 128 * g : 128 * g + 128].astype(f32) if n < R else None
+                    recv_e[x, n, :, lanes].astype(f32) if n < R else None
                     for n in range(3 * t, 3 * t + 3)
                 ]
-                for m in range(min(3, C - 3 * g)):
-                    row = 16 * (3 * g + m)
-                    s6[row : row + 16, 128 * t : 128 * t + 128] = regrouped(held, m).astype(bf16)
-        for c in range(4):
-            cut = slice(256 * c, 256 * c + 256)
-            value = mm(s6[...], t_bwd[:, cut]) + mm(skip_k[...], field[x, :, cut])
-            state = 0.5 * twice_gelu(value + skip_col[...])
+                for m in range(3):
+                    rows = pl.ds(pl.multiple_of(48 * g + 16 * m, 16), 16)
+                    s6[rows, 128 * t : 128 * t + 128] = regrouped(held, m).astype(bf16)
+
+        @pl.loop(0, 4)
+        def _(c):
+            cut = pl.ds(pl.multiple_of(256 * c, 256), 256)
+
+            def twice(ref):
+                return jnp.concatenate([ref[...], ref[...]], axis=1)
+
+            value = mm(s6[0:320, :], t_bwd[:, cut]) + mm(skip_k[...], field[x, :, cut])
+            state = 0.5 * twice_gelu(value + twice(skip_col))
             halves = state.reshape(C, 2, 8, 256)
             for h in range(2):
                 inner = mm(hid_k[...], halves[:, h].reshape(160, 256).astype(bf16))
-                weighed = twice_gelu(inner + hid_col[...]) * out_col[...]
+                weighed = twice_gelu(inner + twice(hid_col)) * twice(out_col)
                 part[pl.ds(pl.multiple_of(x * 16, 16) + 8 * h, 8), cut] = jnp.sum(
                     weighed.reshape(HID, 8, 256), axis=0
                 )
@@ -506,7 +546,7 @@
         v((256, 256), bf16),
         v((R, 2, 16, LW), bf16),
         v((2, R, 16, LW), bf16),
-        v((384, 128), f32),
+        v((192, 128), f32),
         v((R, 2, 24, 128), bf16),
         v((2, R, 24, 128), bf16),
         v((384, 128), f32),
@@ -522,10 +562,12 @@
         v((384, 128), f32),
         v((R, 2, 24, 128), bf16),
         v((2, R, 24, 128), bf16),
-        v((384, 128), f32),
+        v((192, 128), f32),
         v((R, 2, 16, LW), bf16),
         v((2, R, 16, LW), bf16),
-        v((320, 384), bf16),
+        v((336, 384), bf16),
+        v((336, 384), f32),
+        v((288, LW), f32),
         v((32, 1024), f32),
         v((256, 128), f32),
         v((R, 32, 128), bf16),
@@ -539,9 +581,9 @@
         v((128, 128), f32),
         v((320, 320), bf16),
         v((512, 160), bf16),
-        v((320, 256), f32),
-        v((512, 256), f32),
-        v((512, 256), f32),
+        v((320, 128), f32),
+        v((512, 128), f32),
+        v((512, 128), f32),
     ]
     one, by_x = [dma((1,))] * 2, [dma((2,))] * 2
     sems = [dma((15,))] + by_x + by_x + one + [dma((3,))] * 3 + one + by_x + by_x + one + one

time: 94.1 us -> 97.2 us (1.033)
  Pallas kernels: 92.5 us -> 95.7 us
    pallas_call x1, Pallas kernels: 92.5 us -> 95.7 us  [local(): pl.pallas_call(kernel, out_shape=jax.ShapeDtypeStruct((100, 128), bf16),...]
where the time goes in v4:
time: 97.2 us; the launch traced here: 97 us
  Pallas kernels  95.7 us (98%)
  local copies, waits for them, and re-layouts  1.35 us (1%)
    pallas_call x1, Pallas kernels, local(): pl.pallas_call(kernel, out_shape=jax.ShapeDtypeStruct((100, 128), bf16),...  95.7 us

profile of v4, /device:TPU:1, one launch (start us, length us, event | category | flops | bytes accessed | tf_op | source)
XLA Modules:
  0.0 97.0 jit_solution(1448250285943171783)
XLA Ops:
  0.0 95.7 %shard_map.217 = bf16[100,128]{1,0:T(8,128)(2,1)} custom-call(bf16[2,320,1024]{2,1,0:T(8,128)(2,1)} %bitcast.11, bf16[3,3,18,800]{3,2,1,0:T(8,128)(2,1)} %bitcast.12, bf16[20,20]{1,0:T(8,128)(2,1)} %refs_2_.1, f32[1,20]{1,0:T(1,128)} %bitcast.16, bf16[20,64]{1,0:T(8,128)(2,1)} %refs_4_.1, f32[1,64]{1,0:T(1,128)} %bitcast.17, bf16[1,64]{1,0:T(2,128)(2,1)} %bitcast.18, ...), custom_call_target="tpu_custom_call" | custom-call | tf_op jit(solution)/shard_map/pallas_call | solution.py:620
  95.7 1.4 %copy.25 = bf16[1,1,100,128]{3,2,1,0:T(8,128)(2,1)} copy(bf16[1,1,100,128]{3,2,1,0:T(8,128)(2,1)} %bitcast.13) | data formatting | bytes 51200

commit v5 on v4

--- a/solution.py
+++ b/solution.py
@@ -22,15 +22,23 @@
 Y = 128
 KZT = MZ * MT
 PK = 18
-G = 7
+G = 6
 R = 8
 LW = G * 128
+WW = 896
 W2 = 2 * C * C
 MESH = pl.DeviceIdType.MESH
 f32 = jnp.float32
 bf16 = jnp.bfloat16
 GA = math.sqrt(2.0 / math.pi)
 GB = GA * 0.044715
+
+
+def lane_of(ch, r, k):
+    if ch < 18:
+        return 128 * (ch // 3) + 64 * r + PK * (ch % 3) + k
+    tile = 2 * (ch - 18) + k // 10
+    return 128 * tile + 64 * r + 54 + k % 10
 
 
 def constants():
@@ -53,30 +61,29 @@
             forward[:, lane + 64] = -np.sin(a) / math.sqrt(Z * T_SIZE)
             backward[lane] = np.cos(a) / math.sqrt(MX * MY * KZT)
             backward[lane + 64] = -np.sin(a) / math.sqrt(MX * MY * KZT)
-    fy = np.arange(MY) - MY // 2
+    order = (3 * np.arange(R)[None, :] + np.arange(3)[:, None]).reshape(-1)
+    fy = order - MY // 2
     c, s = cos_sin(fy[:, None], np.arange(Y)[None, :], Y)
     y_fwd = np.concatenate([c, s], 0) / math.sqrt(Y)
     y_bwd = np.concatenate([c.T, s.T], 0)
-    fx = np.arange(MX) - MX // 2
+    fx = order - MX // 2
     x_fwd = np.zeros((R, 48, 16))
     x_bwd = np.zeros((R, 32, 24))
-    for e in range(R):
-        x = (16 * np.arange(8)[:, None] + 2 * e + np.arange(2)[None, :]).reshape(-1)
-        c, s = cos_sin(fx[:, None], x[None, :], X)
-        x_fwd[e] = np.concatenate([c, s], 0) / math.sqrt(X)
-        x_bwd[e] = np.concatenate([c.T, s.T], 0)
+    for zh in range(R):
+        c, s = cos_sin(fx[:, None], 16 * zh + np.arange(16)[None, :], X)
+        x_fwd[zh] = np.concatenate([c, s], 0) / math.sqrt(X)
+        x_bwd[zh] = np.concatenate([c.T, s.T], 0)
     gather = np.zeros((LW, 128))
     spread = np.zeros((128, LW))
     for ch in range(C):
         for r in range(2):
             for k in range(PK):
-                lane = 128 * (ch // 3) + 64 * r + PK * (ch % 3) + k
-                gather[lane, 64 * r + ch] = 1.0
-                spread[64 * r + ch, lane] = 1.0
-    widen = np.zeros((128, LW))
-    widen_swapped = np.zeros((128, LW))
-    sum_re = np.zeros((LW, 128))
-    sum_im = np.zeros((LW, 128))
+                gather[lane_of(ch, r, k), 64 * r + ch] = 1.0
+                spread[64 * r + ch, lane_of(ch, r, k)] = 1.0
+    widen = np.zeros((128, WW))
+    widen_swapped = np.zeros((128, WW))
+    sum_re = np.zeros((WW, 128))
+    sum_im = np.zeros((WW, 128))
     for r in range(2):
         for ch in range(C):
             for d in range(C):
@@ -123,7 +130,7 @@
         widen, widen_sw, sum_re, sum_im, regroup,
         send_y, recv_y, ya, send_a, recv_a, xa, xb, send_b, recv_b,
         pairs, amat, mix, send_c, recv_c, xc, xd, send_d, recv_d, xe, send_e, recv_e,
-        s6, s1, wide, part, blk, send_f, recv_f, send_g, recv_g, wpad, perm, pick, idrows, square, skip_k, hid_k,
+        s6, part, blk, send_f, recv_f, send_g, recv_g, wpad, perm, pick, idrows, square, skip_k, hid_k,
         skip_col, hid_col, out_col,
         fetched,
         ss_y, rs_y, ss_a, rs_a, ss_b, rs_b, ss_p, rs_p, ls_p, ss_c, rs_c,
@@ -148,23 +155,18 @@
 
     owners = []
     for n in range(3):
-        first = MY * (3 * e + n) + 3 * zh
+        first = MY * (3 * zh + n) + 3 * e
         owners.append((lax.div(first, 9), lax.div(lax.rem(first, 9), 3)))
     sources = []
     for a in range(3):
         first = 9 * i + 3 * a
         jx, jy = lax.div(first, MY), lax.rem(first, MY)
-        sources.append((R * lax.div(jy, 3) + lax.div(jx, 3), lax.rem(jx, 3)))
+        sources.append((R * zh + lax.div(jy, 3), lax.rem(jx, 3)))
 
     barrier = pltpu.get_barrier_semaphore()
     for near in (on_y, on_z, on_e):
         for d in range(1, R):
             pl.semaphore_signal(barrier, inc=1, device_id=near(d)[1], device_id_type=MESH)
-    for other, _ in owners + sources:
-
-        @pl.when(other != i)
-        def _():
-            pl.semaphore_signal(barrier, inc=1, device_id=(other, j), device_id_type=MESH)
 
     fetch = []
     wanted = [
@@ -216,11 +218,11 @@
     def finish_y(x, recv, recv_sem):
         await_bytes(recv.at[x, pl.ds(0, R - 1)], recv_sem.at[x])
 
-    def start_z(x, send, recv, send_sem, recv_sem):
+    def start_e(x, send, recv, send_sem, recv_sem):
         start(
-            on_z, zh, lambda p: send.at[p, x], lambda p: recv.at[x, p], send_sem.at[x], recv_sem.at[x]
+            on_e, e, lambda p: send.at[p, x], lambda p: recv.at[x, p], send_sem.at[x], recv_sem.at[x]
         )
-        recv[x, zh] = send[zh, x]
+        recv[x, e] = send[e, x]
 
     def weights_copy(n, a, device):
         return pltpu.make_async_remote_copy(
@@ -274,57 +276,49 @@
 
     lane = iota((1, 128), 1)
     in_half = lane & 63
-    piece = [
-        (in_half >= PK * m) & (in_half < PK * (m + 1)) for m in range(3)
-    ]
     fwd_sign = jnp.where(lane < 64, 1.0, -1.0)
 
-    def regrouped(held, n):
-        total = jnp.zeros(held[0].shape, f32)
-        for m, rows in enumerate(held):
-            if rows is None:
-                continue
-            shift = (PK * (m - n)) % 128
+    def lanes_in(low, high):
+        return (in_half >= low) & (in_half < high)
+
+    def put_together(pieces):
+        total = jnp.zeros(pieces[0][0].shape, f32)
+        for rows, origin, low, high in pieces:
+            shift = (low - origin) % 128
             moved = rows if shift == 0 else pltpu.roll(rows, shift, 1)
-            total = jnp.where(piece[m], moved, total)
+            total = jnp.where(lanes_in(low, high), moved, total)
         return total
 
     def combine(cosines, sines, sign):
         return cosines + sign * pltpu.roll(sines, 64, 1)
 
-    expected = 3 * (R - 1)
-    for other, _ in owners + sources:
-        expected = expected + jnp.where(other != i, 1, 0)
-
-    s1[320:336, :] = jnp.zeros((16, 384), f32)
+    def along_zt(x):
+        got = mm(field[x], t_fwd[...])
+        for t in range(3):
+            rows_of = [got[16 * c : 16 * c + 16, 128 * t : 128 * t + 128] for c in range(C)]
+            for n in range(min(3, R - 3 * t)):
+                for g in range(G):
+                    pieces = [
+                        (rows_of[3 * g + m], PK * n, PK * m, PK * m + PK) for m in range(3)
+                    ]
+                    if g < 4:
+                        cut = 10 * (g % 2)
+                        pieces.append(
+                            (rows_of[18 + g // 2], PK * n + cut, 54, 54 + min(10, PK - cut))
+                        )
+                    send_y[3 * t + n, x, :, 128 * g : 128 * g + 128] = put_together(pieces).astype(
+                        bf16
+                    )
+
     fetch[0].wait()
-
-    @pl.loop(0, 2)
-    def _(x):
-        pltpu.make_async_copy(field_in.at[x], field.at[x], fetched.at[1 + x]).wait()
-        s1[0:320, :] = mm(field[x], t_fwd[...])
-
-        @pl.loop(0, G)
-        def _(g):
-            lanes = pl.ds(pl.multiple_of(128 * g, 128), 128)
-            for t in range(3):
-                held = [
-                    s1[pl.ds(pl.multiple_of(48 * g + 16 * m, 16), 16), 128 * t : 128 * t + 128]
-                    for m in range(3)
-                ]
-                for n in range(min(3, R - 3 * t)):
-                    send_y[3 * t + n, x, :, lanes] = regrouped(held, n).astype(bf16)
-
-        @pl.when(x == 0)
-        def _():
-            pl.semaphore_wait(barrier, expected)
-
-        start_y(x, send_y, recv_y, ss_y, rs_y)
-
-        @pl.when(x == 0)
-        def _():
-            start_weights()
-
+    fetch[1].wait()
+    along_zt(0)
+    pl.semaphore_wait(barrier, 3 * (R - 1))
+    start_y(0, send_y, recv_y, ss_y, rs_y)
+    start_weights()
+    fetch[2].wait()
+    along_zt(1)
+    start_y(1, send_y, recv_y, ss_y, rs_y)
     for copy in fetch[3:]:
         copy.wait()
 
@@ -342,10 +336,10 @@
         return jnp.broadcast_to(jnp.sum(at * values, axis=1, keepdims=True), (rows, 128))
 
     def prepare_clear():
-        wpad[...] = jnp.zeros((288, LW), bf16)
         ya[...] = jnp.zeros((192, 128), f32)
-        xb[...] = jnp.zeros((576, 128), f32)
+        xb[...] = jnp.zeros((448, 128), f32)
         xd[...] = jnp.zeros((384, 128), f32)
+        mix[...] = jnp.zeros((56, 128), f32)
 
     def prepare_rows():
         idrows[...] = jnp.full((8, 256), -1, jnp.int32)
@@ -362,6 +356,12 @@
         name = ((place >> 2) & 7) * 32 + (place >> 5) * 4 + (place & 3)
         pick[...] = one_hot(name == idrows[2:3, 0:128]).T.astype(bf16)
 
+    def prepare_weights():
+        wpad[...] = jnp.zeros((288, WW), bf16)
+        finish_weights()
+        for p in range(9):
+            wpad[32 * p : 32 * p + PK, 0:W2] = weight[p // 3, p % 3]
+
     def prepare_skip():
         square[...] = jnp.zeros((128, 128), f32)
         square[0:C, 0:C] = skip_w[...].astype(f32)
@@ -380,98 +380,96 @@
     prepare_clear()
     prepare_skip()
 
-    @pl.loop(0, 2)
-    def _(x):
+    for x in range(2):
         finish_y(x, recv_y, rs_y)
         got = mm(y_fwd[...], recv_y[x].reshape(Y, LW))
         for g in range(G):
             part_g = got[:, 128 * g : 128 * g + 128]
-            ya[pl.ds(g, MY, stride=8), :] = combine(
-                part_g[0:MY], part_g[MY : 2 * MY], fwd_sign
-            )
+            rows = combine(part_g[0:MY], part_g[MY : 2 * MY], fwd_sign)
+            for m in range(3):
+                ya[pl.ds(G * m + g, R, stride=24), :] = rows[R * m : R * m + R]
         send_a[:, x] = ya[...].astype(bf16).reshape(R, 24, 128)
-        start_z(x, send_a, recv_a, ss_a, rs_a)
-
-    prepare_hidden()
+        start_e(x, send_a, recv_a, ss_a, rs_a)
+    prepare_weights()
     for x in range(2):
         finish_y(x, recv_a, rs_a)
 
+    places = range(3 * G)
     for p in range(R):
         for x in range(2):
             xa[48 * p + 24 * x : 48 * p + 24 * x + 24, :] = recv_a[x, p].astype(f32)
-    used = [8 * a + g for a in range(3) for g in range(G)]
     data = jnp.concatenate(
-        [xa[pl.ds(u, 16, stride=24), :] for u in used], axis=1
+        [xa[pl.ds(u, 16, stride=24), :] for u in places], axis=1
     ).astype(bf16)
-    got = mm(x_fwd[e], data)
-    for n, u in enumerate(used):
-        part_u = got[:, 128 * n : 128 * n + 128]
-        xb[pl.ds(u, MX, stride=24), :] = combine(part_u[0:MX], part_u[MX : 2 * MX], fwd_sign)
+    got = mm(x_fwd[zh], data)
+    for u in places:
+        part_u = got[:, 128 * u : 128 * u + 128]
+        rows = combine(part_u[0:MX], part_u[MX : 2 * MX], fwd_sign)
+        for m in range(3):
+            xb[pl.ds(3 * G * m + u, R, stride=56), :] = rows[R * m : R * m + R]
     for p in range(R):
-        send_b[p] = xb[72 * p : 72 * p + 72, :].astype(bf16)
-    exchange(on_e, e, send_b, recv_b, ss_b, rs_b, beside=prepare_out)
+        send_b[p] = xb[56 * p : 56 * p + 56, :].astype(bf16)
+    exchange(on_z, zh, send_b, recv_b, ss_b, rs_b, beside=prepare_hidden)
     total = recv_b[0].astype(f32)
     for p in range(1, R):
         total = total + recv_b[p].astype(f32)
     pairs[...] = total
-    finish_weights()
+
+    k_row = iota((32, 128), 0)
+    k_half = iota((32, 128), 1) & 63
+    usual = (k_half < 54) & (lax.rem(k_half, PK) == k_row)
+    late = (k_half >= 54) & (k_row < PK)
+    own_k = [
+        one_hot(usual | (late & (k_half - 54 == k_row))),
+        one_hot(usual | (late & (k_half - 44 == k_row))),
+    ] * 2 + [one_hot(usual)] * 2
     for p in range(9):
-        wpad[32 * p : 32 * p + PK, 0:W2] = weight[p // 3, p % 3]
-
-    own_k = one_hot(
-        (iota((32, 128), 1) & 63 < 3 * PK)
-        & (lax.rem(iota((32, 128), 1) & 63, PK) == iota((32, 128), 0))
-    )
-
-    @pl.loop(0, 9)
-    def _(p):
-        rows = pl.ds(pl.multiple_of(32 * p, 32), 32)
-        eight = pairs[pl.ds(pl.multiple_of(8 * p, 8), 8), :]
         for g in range(G):
-            row = jnp.broadcast_to(eight[g : g + 1, :], (32, 128))
-            amat[rows, 128 * g : 128 * g + 128] = (row * own_k).astype(bf16)
-
+            row = jnp.broadcast_to(pairs[G * p + g : G * p + g + 1, :], (32, 128))
+            amat[32 * p : 32 * p + 32, 128 * g : 128 * g + 128] = (row * own_k[g]).astype(bf16)
     compact = mm(amat[...], gather[...]).astype(bf16)
     weights = wpad[...].astype(f32)
     straight = (mm(compact, widen[...]) * weights).astype(bf16)
     crossed = (mm(compact, widen_sw[...]) * weights).astype(bf16)
     mixed = (mm(straight, sum_re[...]) + mm(crossed, sum_im[...])).astype(bf16)
-    wide[...] = mm(mixed, spread[...])
-
-    @pl.loop(0, 9)
-    def _(p):
-        rows = pl.ds(pl.multiple_of(32 * p, 32), 32)
-        sums = [
-            jnp.sum(wide[rows, 128 * g : 128 * g + 128] * own_k, axis=0, keepdims=True)
-            for g in range(G)
-        ]
-        mix[pl.ds(pl.multiple_of(8 * p, 8), 8), :] = jnp.concatenate(
-            sums + [jnp.zeros((1, 128), f32)], axis=0
+    wide = mm(mixed, spread[...])
+    for p in range(9):
+        for g in range(G):
+            tile = wide[32 * p : 32 * p + 32, 128 * g : 128 * g + 128] * own_k[g]
+            mix[G * p + g : G * p + g + 1, :] = jnp.sum(tile, axis=0, keepdims=True)
+    send_c[...] = mix[...].astype(bf16)
+
+    def prepare_late():
+        prepare_out()
+        prepare_rows()
+
+    exchange(on_z, zh, send_c, recv_c, ss_c, rs_c, same=True, beside=prepare_late)
+
+    for p in range(R):
+        xc[56 * p : 56 * p + 56, :] = recv_c[p].astype(f32)
+
+    def by_frequency(ref, first, stride):
+        return jnp.concatenate(
+            [ref[pl.ds(first(m), R, stride=stride), :] for m in range(3)], axis=0
         )
 
-    send_c[...] = mix[...].astype(bf16)
-    exchange(on_e, e, send_c, recv_c, ss_c, rs_c, same=True, beside=prepare_rows)
-
-    for p in range(R):
-        xc[72 * p : 72 * p + 72, :] = recv_c[p].astype(f32)
     data = jnp.concatenate(
-        [xc[pl.ds(u, MX, stride=24), :] for u in used], axis=1
+        [by_frequency(xc, lambda m: 3 * G * m + u, 56) for u in places], axis=1
     ).astype(bf16)
-    got = mm(x_bwd[e], data)
-    for n, u in enumerate(used):
-        part_u = got[:, 128 * n : 128 * n + 128]
+    got = mm(x_bwd[zh], data)
+    for u in places:
+        part_u = got[:, 128 * u : 128 * u + 128]
         xd[pl.ds(u, 16, stride=24), :] = combine(part_u[0:16], part_u[16:32], -fwd_sign)
     for x in range(2):
         for p in range(R):
             send_d[p, x] = xd[48 * p + 24 * x : 48 * p + 24 * x + 24, :].astype(bf16)
-        start_z(x, send_d, recv_d, ss_d, rs_d)
-
-    @pl.loop(0, 2)
-    def _(x):
+        start_e(x, send_d, recv_d, ss_d, rs_d)
+
+    for x in range(2):
         finish_y(x, recv_d, rs_d)
         xe[...] = recv_d[x].astype(f32).reshape(192, 128)
         data = jnp.concatenate(
-            [xe[pl.ds(g, MY, stride=8), :] for g in range(G)], axis=1
+            [by_frequency(xe, lambda m: G * m + g, 24) for g in range(G)], axis=1
         ).astype(bf16)
         got = mm(y_bwd[...], data)
         for g in range(G):
@@ -483,27 +481,31 @@
     @pl.loop(0, 2)
     def _(x):
         finish_y(x, recv_e, rs_e)
-
-        @pl.loop(0, G)
-        def _(g):
-            lanes = pl.ds(pl.multiple_of(128 * g, 128), 128)
-            for t in range(3):
-                held = [
-                    recv_e[x, n, :, lanes].astype(f32) if n < R else None
-                    for n in range(3 * t, 3 * t + 3)
-                ]
-                for m in range(3):
-                    rows = pl.ds(pl.multiple_of(48 * g + 16 * m, 16), 16)
-                    s6[rows, 128 * t : 128 * t + 128] = regrouped(held, m).astype(bf16)
-
-        @pl.loop(0, 4)
-        def _(c):
-            cut = pl.ds(pl.multiple_of(256 * c, 256), 256)
-
-            def twice(ref):
-                return jnp.concatenate([ref[...], ref[...]], axis=1)
-
-            value = mm(s6[0:320, :], t_bwd[:, cut]) + mm(skip_k[...], field[x, :, cut])
+        for t in range(3):
+            rows_of = [
+                [recv_e[x, n, :, 128 * g : 128 * g + 128].astype(f32) for g in range(G)]
+                for n in range(3 * t, min(R, 3 * t + 3))
+            ]
+            for c in range(C):
+                pieces = []
+                for n, tiles in enumerate(rows_of):
+                    if c < 18:
+                        pieces.append((tiles[c // 3], PK * (c % 3), PK * n, PK * n + PK))
+                    else:
+                        for part_k in range(2):
+                            low = PK * n + 10 * part_k
+                            tile = tiles[2 * (c - 18) + part_k]
+                            pieces.append((tile, 54, low, min(low + 10, PK * n + PK)))
+                s6[16 * c : 16 * c + 16, 128 * t : 128 * t + 128] = put_together(pieces).astype(
+                    bf16
+                )
+
+        def twice(ref):
+            return jnp.concatenate([ref[...], ref[...]], axis=1)
+
+        for c in range(4):
+            cut = slice(256 * c, 256 * c + 256)
+            value = mm(s6[...], t_bwd[:, cut]) + mm(skip_k[...], field[x, :, cut])
             state = 0.5 * twice_gelu(value + twice(skip_col))
             halves = state.reshape(C, 2, 8, 256)
             for h in range(2):
@@ -539,10 +541,10 @@
         v((R, 32, 24), bf16),
         v((LW, 128), bf16),
         v((128, LW), bf16),
-        v((128, LW), bf16),
-        v((128, LW), bf16),
-        v((LW, 128), bf16),
-        v((LW, 128), bf16),
+        v((128, WW), bf16),
+        v((128, WW), bf16),
+        v((WW, 128), bf16),
+        v((WW, 128), bf16),
         v((256, 256), bf16),
         v((R, 2, 16, LW), bf16),
         v((2, R, 16, LW), bf16),
@@ -550,31 +552,29 @@
         v((R, 2, 24, 128), bf16),
         v((2, R, 24, 128), bf16),
         v((384, 128), f32),
-        v((576, 128), f32),
-        v((R, 72, 128), bf16),
-        v((R, 72, 128), bf16),
-        v((72, 128), f32),
+        v((448, 128), f32),
+        v((R, 56, 128), bf16),
+        v((R, 56, 128), bf16),
+        v((56, 128), f32),
         v((288, LW), bf16),
-        v((72, 128), f32),
-        v((72, 128), bf16),
-        v((R, 72, 128), bf16),
-        v((576, 128), f32),
+        v((56, 128), f32),
+        v((56, 128), bf16),
+        v((R, 56, 128), bf16),
+        v((448, 128), f32),
         v((384, 128), f32),
         v((R, 2, 24, 128), bf16),
         v((2, R, 24, 128), bf16),
         v((192, 128), f32),
         v((R, 2, 16, LW), bf16),
         v((2, R, 16, LW), bf16),
-        v((336, 384), bf16),
-        v((336, 384), f32),
-        v((288, LW), f32),
+        v((320, 384), bf16),
         v((32, 1024), f32),
         v((256, 128), f32),
         v((R, 32, 128), bf16),
         v((R, 32, 128), bf16),
         v((R, 32, 128), bf16),
         v((R, 32, 128), bf16),
-        v((288, LW), bf16),
+        v((288, WW), bf16),
         v((256, 256), bf16),
         v((128, 256), bf16),
         v((8, 256), jnp.int32),

time: 97.2 us -> 75 us (0.77)
  Pallas kernels: 95.7 us -> 73.4 us
    pallas_call x1, Pallas kernels: 95.7 us -> 73.4 us  [local(): pl.pallas_call(kernel, out_shape=jax.ShapeDtypeStruct((100, 128), bf16),...]
where the time goes in v5:
time: 75 us; the launch traced here: 74.8 us
  Pallas kernels  73.4 us (98%)
  local copies, waits for them, and re-layouts  1.35 us (2%)
    pallas_call x1, Pallas kernels, local(): pl.pallas_call(kernel, out_shape=jax.ShapeDtypeStruct((100, 128), bf16),...  73.4 us

profile of v5, /device:TPU:1, one launch (start us, length us, event | category | flops | bytes accessed | tf_op | source)
XLA Modules:
  0.0 74.8 jit_solution(17090664741565353992)
XLA Ops:
  0.0 73.4 %shard_map.217 = bf16[100,128]{1,0:T(8,128)(2,1)} custom-call(bf16[2,320,1024]{2,1,0:T(8,128)(2,1)} %bitcast.11, bf16[3,3,18,800]{3,2,1,0:T(8,128)(2,1)} %bitcast.12, bf16[20,20]{1,0:T(8,128)(2,1)} %refs_2_.1, f32[1,20]{1,0:T(1,128)} %bitcast.16, bf16[20,64]{1,0:T(8,128)(2,1)} %refs_4_.1, f32[1,64]{1,0:T(1,128)} %bitcast.17, bf16[1,64]{1,0:T(2,128)(2,1)} %bitcast.18, ...), custom_call_target="tpu_custom_call" | custom-call | tf_op jit(solution)/shard_map/pallas_call | solution.py:620
  73.4 1.4 %copy.25 = bf16[1,1,100,128]{3,2,1,0:T(8,128)(2,1)} copy(bf16[1,1,100,128]{3,2,1,0:T(8,128)(2,1)} %bitcast.13) | data formatting | bytes 51200

commit v6 on v5

--- a/solution.py
+++ b/solution.py
@@ -27,6 +27,8 @@
 LW = G * 128
 WW = 896
 W2 = 2 * C * C
+BIAS_LANE = 60
+FAR_FIRST = (4, 3, 5, 2, 6, 1, 7)
 MESH = pl.DeviceIdType.MESH
 f32 = jnp.float32
 bf16 = jnp.bfloat16
@@ -61,6 +63,7 @@
             forward[:, lane + 64] = -np.sin(a) / math.sqrt(Z * T_SIZE)
             backward[lane] = np.cos(a) / math.sqrt(MX * MY * KZT)
             backward[lane + 64] = -np.sin(a) / math.sqrt(MX * MY * KZT)
+    backward[BIAS_LANE : BIAS_LANE + 3] = 1.0
     order = (3 * np.arange(R)[None, :] + np.arange(3)[:, None]).reshape(-1)
     fy = order - MY // 2
     c, s = cos_sin(fy[:, None], np.arange(Y)[None, :], Y)
@@ -131,7 +134,7 @@
         send_y, recv_y, ya, send_a, recv_a, xa, xb, send_b, recv_b,
         pairs, amat, mix, send_c, recv_c, xc, xd, send_d, recv_d, xe, send_e, recv_e,
         s6, part, blk, send_f, recv_f, send_g, recv_g, wpad, perm, pick, idrows, square, skip_k, hid_k,
-        skip_col, hid_col, out_col,
+        skip_bias, out_k,
         fetched,
         ss_y, rs_y, ss_a, rs_a, ss_b, rs_b, ss_p, rs_p, ls_p, ss_c, rs_c,
         ss_d, rs_d, ss_e, rs_e, ss_f, rs_f, ss_g, rs_g,
@@ -186,7 +189,7 @@
         pltpu.make_async_copy(view, view, sem).wait()
 
     def start(near, me, send, recv, send_sem, recv_sem):
-        for d in range(1, R):
+        for d in FAR_FIRST:
             peer, device = near(d)
             pltpu.make_async_remote_copy(
                 src_ref=send(peer),
@@ -281,8 +284,9 @@
     def lanes_in(low, high):
         return (in_half >= low) & (in_half < high)
 
-    def put_together(pieces):
-        total = jnp.zeros(pieces[0][0].shape, f32)
+    def put_together(pieces, total=None):
+        if total is None:
+            total = jnp.zeros(pieces[0][0].shape, f32)
         for rows, origin, low, high in pieces:
             shift = (low - origin) % 128
             moved = rows if shift == 0 else pltpu.roll(rows, shift, 1)
@@ -328,7 +332,14 @@
         right = one_hot((iota((128, cols), 1) >> shift) == iota((128, cols), 0)).astype(bf16)
         wide = mm(mm(left, values.T.astype(bf16)).astype(bf16), right)
         same = (iota((rows, cols), 0) & (places - 1)) == (iota((rows, cols), 1) & (places - 1))
-        return jnp.where(same, wide, 0.0).astype(bf16)
+        return jnp.where(same, wide, 0.0)
+
+    def with_parts(matrix, values, at, first):
+        for n in range(3):
+            half = values.astype(bf16).astype(f32)
+            matrix = jnp.where(at == first + n, half, matrix)
+            values = values - half
+        return matrix
 
     def column(values, places, width, rows):
         shift = places.bit_length() - 1
@@ -365,17 +376,24 @@
     def prepare_skip():
         square[...] = jnp.zeros((128, 128), f32)
         square[0:C, 0:C] = skip_w[...].astype(f32)
-        skip_k[...] = spread_map(square[...], 320, 320, 16)
-        skip_col[...] = column(skip_b[...], 16, C, 320)
+        skip_k[...] = spread_map(square[...], 320, 320, 16).astype(bf16)
+        skip_bias[...] = with_parts(
+            jnp.zeros((320, 128), f32), column(skip_b[...], 16, C, 320), iota((320, 128), 1), BIAS_LANE
+        )
 
     def prepare_hidden():
         square[...] = jnp.zeros((128, 128), f32)
-        square[0:C, 0:HID] = hid_w[...].astype(f32)
-        hid_k[...] = spread_map(square[...], 512, 160, 8)
-        hid_col[...] = column(hid_b[...], 8, HID, 512)
+        square[0:C, 0:HID] = 0.5 * hid_w[...].astype(f32)
+        wide = spread_map(square[...], 512, 176, 8)
+        bias = column(hid_b[...], 8, HID, 512)
+        bias = jnp.concatenate([bias, bias[:, 0:48]], axis=1)
+        hid_k[...] = with_parts(wide, bias, iota((512, 176), 1), 160).astype(bf16)
 
     def prepare_out():
-        out_col[...] = column(0.5 * out_w[...].astype(f32), 8, HID, 512)
+        right = one_hot((iota((HID, 512), 1) >> 3) == iota((HID, 512), 0)).astype(bf16)
+        left = jnp.broadcast_to(0.5 * out_w[...].astype(f32), (16, HID)).astype(bf16)
+        same = (iota((16, 512), 1) & 7) == iota((16, 512), 0)
+        out_k[...] = jnp.where(same, mm(left, right), 0.0).astype(bf16)
 
     prepare_clear()
     prepare_skip()
@@ -496,24 +514,20 @@
                             low = PK * n + 10 * part_k
                             tile = tiles[2 * (c - 18) + part_k]
                             pieces.append((tile, 54, low, min(low + 10, PK * n + PK)))
-                s6[16 * c : 16 * c + 16, 128 * t : 128 * t + 128] = put_together(pieces).astype(
-                    bf16
-                )
-
-        def twice(ref):
-            return jnp.concatenate([ref[...], ref[...]], axis=1)
+                bias = skip_bias[16 * c : 16 * c + 16, :] if t == 0 else None
+                s6[16 * c : 16 * c + 16, 128 * t : 128 * t + 128] = put_together(
+                    pieces, bias
+                ).astype(bf16)
 
         for c in range(4):
             cut = slice(256 * c, 256 * c + 256)
             value = mm(s6[...], t_bwd[:, cut]) + mm(skip_k[...], field[x, :, cut])
-            state = 0.5 * twice_gelu(value + twice(skip_col))
-            halves = state.reshape(C, 2, 8, 256)
+            halves = value.reshape(C, 2, 8, 256)
             for h in range(2):
-                inner = mm(hid_k[...], halves[:, h].reshape(160, 256).astype(bf16))
-                weighed = twice_gelu(inner + twice(hid_col)) * twice(out_col)
-                part[pl.ds(pl.multiple_of(x * 16, 16) + 8 * h, 8), cut] = jnp.sum(
-                    weighed.reshape(HID, 8, 256), axis=0
-                )
+                state = twice_gelu(halves[:, h].reshape(160, 256).astype(bf16))
+                state = jnp.concatenate([state, jnp.ones((16, 256), bf16)], axis=0)
+                hidden = twice_gelu(mm(hid_k[...], state).astype(bf16))
+                part[pl.ds(pl.multiple_of(x * 16, 16) + 8 * h, 8), cut] = mm(out_k[...], hidden)[0:8]
 
     for b in range(8):
         blk[pl.ds(b, 32, stride=8), :] = part[:, 128 * b : 128 * b + 128]
@@ -580,10 +594,9 @@
         v((8, 256), jnp.int32),
         v((128, 128), f32),
         v((320, 320), bf16),
-        v((512, 160), bf16),
+        v((512, 176), bf16),
         v((320, 128), f32),
-        v((512, 128), f32),
-        v((512, 128), f32),
+        v((16, 512), bf16),
     ]
     one, by_x = [dma((1,))] * 2, [dma((2,))] * 2
     sems = [dma((15,))] + by_x + by_x + one + [dma((3,))] * 3 + one + by_x + by_x + one + one

time: 75 us -> 74.1 us (0.988)
  Pallas kernels: 73.4 us -> 72.5 us
    pallas_call x1, Pallas kernels: 73.4 us -> 72.5 us  [local(): pl.pallas_call(kernel, out_shape=jax.ShapeDtypeStruct((100, 128), bf16),...]
where the time goes in v6:
time: 74.1 us; the launch traced here: 73.8 us
  Pallas kernels  72.5 us (98%)
  local copies, waits for them, and re-layouts  1.35 us (2%)
    pallas_call x1, Pallas kernels, local(): pl.pallas_call(kernel, out_shape=jax.ShapeDtypeStruct((100, 128), bf16),...  72.5 us

profile of v6, /device:TPU:1, one launch (start us, length us, event | category | flops | bytes accessed | tf_op | source)
XLA Modules:
  0.0 73.8 jit_solution(13464001234453004600)
XLA Ops:
  0.0 72.5 %shard_map.217 = bf16[100,128]{1,0:T(8,128)(2,1)} custom-call(bf16[2,320,1024]{2,1,0:T(8,128)(2,1)} %bitcast.11, bf16[3,3,18,800]{3,2,1,0:T(8,128)(2,1)} %bitcast.12, bf16[20,20]{1,0:T(8,128)(2,1)} %refs_2_.1, f32[1,20]{1,0:T(1,128)} %bitcast.16, bf16[20,64]{1,0:T(8,128)(2,1)} %refs_4_.1, f32[1,64]{1,0:T(1,128)} %bitcast.17, bf16[1,64]{1,0:T(2,128)(2,1)} %bitcast.18, ...), custom_call_target="tpu_custom_call" | custom-call | tf_op jit(solution)/shard_map/pallas_call | solution.py:633
  72.5 1.4 %copy.25 = bf16[1,1,100,128]{3,2,1,0:T(8,128)(2,1)} copy(bf16[1,1,100,128]{3,2,1,0:T(8,128)(2,1)} %bitcast.13) | data formatting | bytes 51200

commit v7 on v6

--- a/solution.py
+++ b/solution.py
@@ -25,6 +25,7 @@
 G = 6
 R = 8
 LW = G * 128
+LS = LW // 2
 WW = 896
 W2 = 2 * C * C
 BIAS_LANE = 60
@@ -73,7 +74,8 @@
     x_fwd = np.zeros((R, 48, 16))
     x_bwd = np.zeros((R, 32, 24))
     for zh in range(R):
-        c, s = cos_sin(fx[:, None], 16 * zh + np.arange(16)[None, :], X)
+        x = (16 * zh + 2 * np.arange(R)[None, :] + np.arange(2)[:, None]).reshape(-1)
+        c, s = cos_sin(fx[:, None], x[None, :], X)
         x_fwd[zh] = np.concatenate([c, s], 0) / math.sqrt(X)
         x_bwd[zh] = np.concatenate([c.T, s.T], 0)
     gather = np.zeros((LW, 128))
@@ -183,8 +185,6 @@
         fetch.append(pltpu.make_async_copy(source, target, fetched.at[n]))
         fetch[n].start()
 
-    sent = []
-
     def await_bytes(view, sem):
         pltpu.make_async_copy(view, view, sem).wait()
 
@@ -200,32 +200,18 @@
                 device_id_type=MESH,
             ).start()
 
-    def exchange(near, me, send, recv, send_sem, recv_sem, same=False, beside=None):
+    def trade(near, me, s, send, recv, send_sem, recv_sem):
         start(
-            near, me, (lambda p: send) if same else (lambda p: send.at[p]), lambda p: recv.at[p],
-            send_sem.at[0], recv_sem.at[0],
+            near, me, lambda p: send.at[p, s], lambda p: recv.at[s, p], send_sem.at[s], recv_sem.at[s]
         )
-        recv[me] = send[...] if same else send[me]
-        seven = recv.at[pl.ds(0, R - 1)]
-        sent.append((seven, send_sem.at[0]))
-        if beside is not None:
-            beside()
-        await_bytes(seven, recv_sem.at[0])
-
-    def start_y(x, send, recv, send_sem, recv_sem):
-        start(
-            on_y, j, lambda p: send.at[p, x], lambda p: recv.at[x, p], send_sem.at[x], recv_sem.at[x]
-        )
-        recv[x, j] = send[j, x]
-
-    def finish_y(x, recv, recv_sem):
-        await_bytes(recv.at[x, pl.ds(0, R - 1)], recv_sem.at[x])
-
-    def start_e(x, send, recv, send_sem, recv_sem):
-        start(
-            on_e, e, lambda p: send.at[p, x], lambda p: recv.at[x, p], send_sem.at[x], recv_sem.at[x]
-        )
-        recv[x, e] = send[e, x]
+        pltpu.make_async_copy(send.at[me, s], recv.at[s, me], recv_sem.at[s]).start()
+
+    def trade_same(near, me, s, send, recv, send_sem, recv_sem):
+        start(near, me, lambda p: send.at[s], lambda p: recv.at[s, p], send_sem.at[s], recv_sem.at[s])
+        pltpu.make_async_copy(send.at[s], recv.at[s, me], recv_sem.at[s]).start()
+
+    def finish(s, recv, recv_sem):
+        await_bytes(recv.at[s], recv_sem.at[s])
 
     def weights_copy(n, a, device):
         return pltpu.make_async_remote_copy(
@@ -271,11 +257,12 @@
             def _():
                 weights_copy(n, a, device).wait_send()
 
-        for view, sem in sent:
-            await_bytes(view, sem)
-        for recv, send_sem in ((recv_y, ss_y), (recv_a, ss_a), (recv_d, ss_d), (recv_e, ss_e)):
-            for x in range(2):
-                await_bytes(recv.at[x, pl.ds(0, R - 1)], send_sem.at[x])
+        for recv, send_sem in (
+            (recv_y, ss_y), (recv_a, ss_a), (recv_b, ss_b), (recv_c, ss_c), (recv_d, ss_d),
+            (recv_e, ss_e), (recv_f, ss_f), (recv_g, ss_g),
+        ):
+            for n in range(recv.shape[0]):
+                await_bytes(recv.at[n, pl.ds(0, R - 1)], send_sem.at[n])
 
     lane = iota((1, 128), 1)
     in_half = lane & 63
@@ -296,33 +283,48 @@
     def combine(cosines, sines, sign):
         return cosines + sign * pltpu.roll(sines, 64, 1)
 
-    def along_zt(x):
-        got = mm(field[x], t_fwd[...])
-        for t in range(3):
-            rows_of = [got[16 * c : 16 * c + 16, 128 * t : 128 * t + 128] for c in range(C)]
-            for n in range(min(3, R - 3 * t)):
-                for g in range(G):
+    rows_of = {}
+
+    def along_zt(channels):
+        runs = []
+        for x in range(2):
+            for low, high in channels:
+                runs.append(field[x, 16 * low : 16 * high, :])
+        got = mm(jnp.concatenate(runs, axis=0), t_fwd[...])
+        row = 0
+        for x in range(2):
+            for low, high in channels:
+                for c in range(low, high):
+                    rows_of[x, c] = got[row : row + 16]
+                    row += 16
+
+    def place_zt(s):
+        for x in range(2):
+            for j_to in range(R):
+                t, n = j_to // 3, j_to % 3
+                lanes = slice(128 * t, 128 * t + 128)
+                for g in range(3 * s, 3 * s + 3):
                     pieces = [
-                        (rows_of[3 * g + m], PK * n, PK * m, PK * m + PK) for m in range(3)
+                        (rows_of[x, 3 * g + m][:, lanes], PK * n, PK * m, PK * m + PK)
+                        for m in range(3)
                     ]
                     if g < 4:
                         cut = 10 * (g % 2)
-                        pieces.append(
-                            (rows_of[18 + g // 2], PK * n + cut, 54, 54 + min(10, PK - cut))
-                        )
-                    send_y[3 * t + n, x, :, 128 * g : 128 * g + 128] = put_together(pieces).astype(
-                        bf16
-                    )
-
-    fetch[0].wait()
-    fetch[1].wait()
-    along_zt(0)
+                        last = rows_of[x, 18 + g // 2][:, lanes]
+                        pieces.append((last, PK * n + cut, 54, 54 + min(10, PK - cut)))
+                    at = 128 * (g - 3 * s)
+                    send_y[j_to, s, x, :, at : at + 128] = put_together(pieces).astype(bf16)
+
+    for n in range(3):
+        fetch[n].wait()
+    along_zt([(0, 9), (18, 20)])
+    place_zt(0)
     pl.semaphore_wait(barrier, 3 * (R - 1))
-    start_y(0, send_y, recv_y, ss_y, rs_y)
+    trade(on_y, j, 0, send_y, recv_y, ss_y, rs_y)
     start_weights()
-    fetch[2].wait()
-    along_zt(1)
-    start_y(1, send_y, recv_y, ss_y, rs_y)
+    along_zt([(9, 18)])
+    place_zt(1)
+    trade(on_y, j, 1, send_y, recv_y, ss_y, rs_y)
     for copy in fetch[3:]:
         copy.wait()
 
@@ -347,10 +349,8 @@
         return jnp.broadcast_to(jnp.sum(at * values, axis=1, keepdims=True), (rows, 128))
 
     def prepare_clear():
-        ya[...] = jnp.zeros((192, 128), f32)
-        xb[...] = jnp.zeros((448, 128), f32)
-        xd[...] = jnp.zeros((384, 128), f32)
-        mix[...] = jnp.zeros((56, 128), f32)
+        for ref in (ya, xb, xd, mix):
+            ref[...] = jnp.zeros(ref.shape, f32)
 
     def prepare_rows():
         idrows[...] = jnp.full((8, 256), -1, jnp.int32)
@@ -398,40 +398,54 @@
     prepare_clear()
     prepare_skip()
 
-    for x in range(2):
-        finish_y(x, recv_y, rs_y)
-        got = mm(y_fwd[...], recv_y[x].reshape(Y, LW))
-        for g in range(G):
-            part_g = got[:, 128 * g : 128 * g + 128]
-            rows = combine(part_g[0:MY], part_g[MY : 2 * MY], fwd_sign)
+    def along_y(s):
+        finish(s, recv_y, rs_y)
+        data = jnp.concatenate(
+            [recv_y[s, :, x].reshape(Y, LS) for x in range(2)], axis=1
+        )
+        got = mm(y_fwd[...], data)
+        for x in range(2):
+            for g in range(3):
+                part_g = got[:, LS * x + 128 * g : LS * x + 128 * g + 128]
+                rows = combine(part_g[0:MY], part_g[MY : 2 * MY], fwd_sign)
+                for m in range(3):
+                    ya[pl.ds(9 * x + 3 * m + g, R, stride=24), :] = rows[R * m : R * m + R]
+        send_a[:, s] = ya[...].astype(bf16).reshape(R, 24, 128)
+        trade(on_e, e, s, send_a, recv_a, ss_a, rs_a)
+
+    def along_x(s):
+        finish(s, recv_a, rs_a)
+        xa[...] = recv_a[s].astype(f32).reshape(192, 128)
+        data = jnp.concatenate(
+            [
+                jnp.concatenate(
+                    [xa[pl.ds(9 * x + u, R, stride=24), :] for x in range(2)], axis=0
+                )
+                for u in range(9)
+            ],
+            axis=1,
+        ).astype(bf16)
+        got = mm(x_fwd[zh], data)
+        for u in range(9):
+            part_u = got[:, 128 * u : 128 * u + 128]
+            rows = combine(part_u[0:MX], part_u[MX : 2 * MX], fwd_sign)
             for m in range(3):
-                ya[pl.ds(G * m + g, R, stride=24), :] = rows[R * m : R * m + R]
-        send_a[:, x] = ya[...].astype(bf16).reshape(R, 24, 128)
-        start_e(x, send_a, recv_a, ss_a, rs_a)
+                xb[pl.ds(9 * m + u, R, stride=32), :] = rows[R * m : R * m + R]
+        send_b[:, s] = xb[...].astype(bf16).reshape(R, 32, 128)
+        trade(on_z, zh, s, send_b, recv_b, ss_b, rs_b)
+
+    along_y(0)
+    along_x(0)
+    along_y(1)
     prepare_weights()
-    for x in range(2):
-        finish_y(x, recv_a, rs_a)
-
-    places = range(3 * G)
-    for p in range(R):
-        for x in range(2):
-            xa[48 * p + 24 * x : 48 * p + 24 * x + 24, :] = recv_a[x, p].astype(f32)
-    data = jnp.concatenate(
-        [xa[pl.ds(u, 16, stride=24), :] for u in places], axis=1
-    ).astype(bf16)
-    got = mm(x_fwd[zh], data)
-    for u in places:
-        part_u = got[:, 128 * u : 128 * u + 128]
-        rows = combine(part_u[0:MX], part_u[MX : 2 * MX], fwd_sign)
-        for m in range(3):
-            xb[pl.ds(3 * G * m + u, R, stride=56), :] = rows[R * m : R * m + R]
-    for p in range(R):
-        send_b[p] = xb[56 * p : 56 * p + 56, :].astype(bf16)
-    exchange(on_z, zh, send_b, recv_b, ss_b, rs_b, beside=prepare_hidden)
-    total = recv_b[0].astype(f32)
-    for p in range(1, R):
-        total = total + recv_b[p].astype(f32)
-    pairs[...] = total
+    along_x(1)
+    prepare_hidden()
+    for s in range(2):
+        finish(s, recv_b, rs_b)
+        total = recv_b[s, 0].astype(f32)
+        for p in range(1, R):
+            total = total + recv_b[s, p].astype(f32)
+        pairs[s] = total
 
     k_row = iota((32, 128), 0)
     k_half = iota((32, 128), 1) & 63
@@ -443,100 +457,113 @@
     ] * 2 + [one_hot(usual)] * 2
     for p in range(9):
         for g in range(G):
-            row = jnp.broadcast_to(pairs[G * p + g : G * p + g + 1, :], (32, 128))
+            row = jnp.broadcast_to(pairs[g // 3, 3 * p + g % 3 : 3 * p + g % 3 + 1, :], (32, 128))
             amat[32 * p : 32 * p + 32, 128 * g : 128 * g + 128] = (row * own_k[g]).astype(bf16)
     compact = mm(amat[...], gather[...]).astype(bf16)
     weights = wpad[...].astype(f32)
     straight = (mm(compact, widen[...]) * weights).astype(bf16)
     crossed = (mm(compact, widen_sw[...]) * weights).astype(bf16)
     mixed = (mm(straight, sum_re[...]) + mm(crossed, sum_im[...])).astype(bf16)
-    wide = mm(mixed, spread[...])
-    for p in range(9):
-        for g in range(G):
-            tile = wide[32 * p : 32 * p + 32, 128 * g : 128 * g + 128] * own_k[g]
-            mix[G * p + g : G * p + g + 1, :] = jnp.sum(tile, axis=0, keepdims=True)
-    send_c[...] = mix[...].astype(bf16)
-
-    def prepare_late():
-        prepare_out()
-        prepare_rows()
-
-    exchange(on_z, zh, send_c, recv_c, ss_c, rs_c, same=True, beside=prepare_late)
-
-    for p in range(R):
-        xc[56 * p : 56 * p + 56, :] = recv_c[p].astype(f32)
+    for s in range(2):
+        wide = mm(mixed, spread[:, LS * s : LS * s + LS])
+        for p in range(9):
+            for g in range(3):
+                tile = wide[32 * p : 32 * p + 32, 128 * g : 128 * g + 128] * own_k[3 * s + g]
+                mix[s, 3 * p + g : 3 * p + g + 1, :] = jnp.sum(tile, axis=0, keepdims=True)
+        send_c[s] = mix[s].astype(bf16)
+        trade_same(on_z, zh, s, send_c, recv_c, ss_c, rs_c)
+    prepare_out()
+    prepare_rows()
 
     def by_frequency(ref, first, stride):
         return jnp.concatenate(
             [ref[pl.ds(first(m), R, stride=stride), :] for m in range(3)], axis=0
         )
 
-    data = jnp.concatenate(
-        [by_frequency(xc, lambda m: 3 * G * m + u, 56) for u in places], axis=1
-    ).astype(bf16)
-    got = mm(x_bwd[zh], data)
-    for u in places:
-        part_u = got[:, 128 * u : 128 * u + 128]
-        xd[pl.ds(u, 16, stride=24), :] = combine(part_u[0:16], part_u[16:32], -fwd_sign)
-    for x in range(2):
-        for p in range(R):
-            send_d[p, x] = xd[48 * p + 24 * x : 48 * p + 24 * x + 24, :].astype(bf16)
-        start_e(x, send_d, recv_d, ss_d, rs_d)
-
-    for x in range(2):
-        finish_y(x, recv_d, rs_d)
-        xe[...] = recv_d[x].astype(f32).reshape(192, 128)
+    def back_x(s):
+        finish(s, recv_c, rs_c)
+        xc[...] = recv_c[s].astype(f32).reshape(256, 128)
         data = jnp.concatenate(
-            [by_frequency(xe, lambda m: G * m + g, 24) for g in range(G)], axis=1
+            [by_frequency(xc, lambda m: 9 * m + u, 32) for u in range(9)], axis=1
         ).astype(bf16)
-        got = mm(y_bwd[...], data)
-        for g in range(G):
-            part_g = got[:, 128 * g : 128 * g + 128]
-            turned = combine(part_g[0:Y], part_g[Y : 2 * Y], -fwd_sign).astype(bf16)
-            send_e[:, x, :, 128 * g : 128 * g + 128] = turned.reshape(R, 16, 128)
-        start_y(x, send_e, recv_e, ss_e, rs_e)
-
-    @pl.loop(0, 2)
-    def _(x):
-        finish_y(x, recv_e, rs_e)
+        got = mm(x_bwd[zh], data)
+        for u in range(9):
+            part_u = got[:, 128 * u : 128 * u + 128]
+            rows = combine(part_u[0:16], part_u[16:32], -fwd_sign)
+            for x in range(2):
+                xd[pl.ds(9 * x + u, R, stride=24), :] = rows[R * x : R * x + R]
+        send_d[:, s] = xd[...].astype(bf16).reshape(R, 24, 128)
+        trade(on_e, e, s, send_d, recv_d, ss_d, rs_d)
+
+    def back_y(s):
+        finish(s, recv_d, rs_d)
+        xe[...] = recv_d[s].astype(f32).reshape(192, 128)
+        for x in range(2):
+            data = jnp.concatenate(
+                [by_frequency(xe, lambda m: 9 * x + 3 * m + g, 24) for g in range(3)], axis=1
+            ).astype(bf16)
+            got = mm(y_bwd[...], data)
+            for g in range(3):
+                part_g = got[:, 128 * g : 128 * g + 128]
+                turned = combine(part_g[0:Y], part_g[Y : 2 * Y], -fwd_sign).astype(bf16)
+                send_e[:, 2 * s + x, :, 128 * g : 128 * g + 128] = turned.reshape(R, 16, 128)
+            trade(on_y, j, 2 * s + x, send_e, recv_e, ss_e, rs_e)
+
+    back_x(0)
+    back_y(0)
+    back_x(1)
+    back_y(1)
+
+    def columns(x, s, channels):
         for t in range(3):
-            rows_of = [
-                [recv_e[x, n, :, 128 * g : 128 * g + 128].astype(f32) for g in range(G)]
-                for n in range(3 * t, min(R, 3 * t + 3))
-            ]
-            for c in range(C):
+            tiles = {}
+            for n in range(3 * t, min(R, 3 * t + 3)):
+                for g in range(3 * s + 3):
+                    at = 128 * (g % 3)
+                    tiles[n - 3 * t, g] = recv_e[2 * (g // 3) + x, n, :, at : at + 128].astype(f32)
+            for c in channels:
                 pieces = []
-                for n, tiles in enumerate(rows_of):
+                for n in range(min(3, R - 3 * t)):
                     if c < 18:
-                        pieces.append((tiles[c // 3], PK * (c % 3), PK * n, PK * n + PK))
+                        pieces.append((tiles[n, c // 3], PK * (c % 3), PK * n, PK * n + PK))
                     else:
                         for part_k in range(2):
                             low = PK * n + 10 * part_k
-                            tile = tiles[2 * (c - 18) + part_k]
+                            tile = tiles[n, 2 * (c - 18) + part_k]
                             pieces.append((tile, 54, low, min(low + 10, PK * n + PK)))
                 bias = skip_bias[16 * c : 16 * c + 16, :] if t == 0 else None
-                s6[16 * c : 16 * c + 16, 128 * t : 128 * t + 128] = put_together(
+                s6[x, 16 * c : 16 * c + 16, 128 * t : 128 * t + 128] = put_together(
                     pieces, bias
                 ).astype(bf16)
 
+    for x in range(2):
+        finish(x, recv_e, rs_e)
+        columns(x, 0, [*range(9), 18])
+
+    @pl.loop(0, 2)
+    def _(x):
+        finish(2 + x, recv_e, rs_e)
+        columns(x, 1, [*range(9, 18), 19])
         for c in range(4):
             cut = slice(256 * c, 256 * c + 256)
-            value = mm(s6[...], t_bwd[:, cut]) + mm(skip_k[...], field[x, :, cut])
+            value = mm(s6[x], t_bwd[:, cut]) + mm(skip_k[...], field[x, :, cut])
             halves = value.reshape(C, 2, 8, 256)
             for h in range(2):
-                state = twice_gelu(halves[:, h].reshape(160, 256).astype(bf16))
+                state = twice_gelu(halves[:, h].reshape(160, 256)).astype(bf16)
                 state = jnp.concatenate([state, jnp.ones((16, 256), bf16)], axis=0)
-                hidden = twice_gelu(mm(hid_k[...], state).astype(bf16))
+                hidden = twice_gelu(mm(hid_k[...], state)).astype(bf16)
                 part[pl.ds(pl.multiple_of(x * 16, 16) + 8 * h, 8), cut] = mm(out_k[...], hidden)[0:8]
 
     for b in range(8):
         blk[pl.ds(b, 32, stride=8), :] = part[:, 128 * b : 128 * b + 128]
 
-    send_f[...] = mm(perm[...], blk[...].astype(bf16)).astype(bf16).reshape(R, 32, 128)
-    exchange(on_z, zh, send_f, recv_f, ss_f, rs_f)
-    send_g[...] = mm(regroup[...], recv_f[...].reshape(256, 128)).astype(bf16).reshape(R, 32, 128)
-    exchange(on_e, e, send_g, recv_g, ss_g, rs_g)
-    owned = mm(pick[...], recv_g[...].reshape(256, 128))
+    send_f[:, 0] = mm(perm[...], blk[...].astype(bf16)).astype(bf16).reshape(R, 32, 128)
+    trade(on_z, zh, 0, send_f, recv_f, ss_f, rs_f)
+    finish(0, recv_f, rs_f)
+    send_g[:, 0] = mm(regroup[...], recv_f[0].reshape(256, 128)).astype(bf16).reshape(R, 32, 128)
+    trade(on_e, e, 0, send_g, recv_g, ss_g, rs_g)
+    finish(0, recv_g, rs_g)
+    owned = mm(pick[...], recv_g[0].reshape(256, 128))
     out[...] = owned[0:100].astype(bf16)
     finish_sends()
 
@@ -560,34 +587,34 @@
         v((WW, 128), bf16),
         v((WW, 128), bf16),
         v((256, 256), bf16),
-        v((R, 2, 16, LW), bf16),
-        v((2, R, 16, LW), bf16),
+        v((R, 2, 2, 16, LS), bf16),
+        v((2, R, 2, 16, LS), bf16),
         v((192, 128), f32),
         v((R, 2, 24, 128), bf16),
         v((2, R, 24, 128), bf16),
-        v((384, 128), f32),
-        v((448, 128), f32),
-        v((R, 56, 128), bf16),
-        v((R, 56, 128), bf16),
-        v((56, 128), f32),
+        v((192, 128), f32),
+        v((256, 128), f32),
+        v((R, 2, 32, 128), bf16),
+        v((2, R, 32, 128), bf16),
+        v((2, 32, 128), f32),
         v((288, LW), bf16),
-        v((56, 128), f32),
-        v((56, 128), bf16),
-        v((R, 56, 128), bf16),
-        v((448, 128), f32),
-        v((384, 128), f32),
+        v((2, 32, 128), f32),
+        v((2, 32, 128), bf16),
+        v((2, R, 32, 128), bf16),
+        v((256, 128), f32),
+        v((192, 128), f32),
         v((R, 2, 24, 128), bf16),
         v((2, R, 24, 128), bf16),
         v((192, 128), f32),
-        v((R, 2, 16, LW), bf16),
-        v((2, R, 16, LW), bf16),
-        v((320, 384), bf16),
+        v((R, 4, 16, LS), bf16),
+        v((4, R, 16, LS), bf16),
+        v((2, 320, 384), bf16),
         v((32, 1024), f32),
         v((256, 128), f32),
-        v((R, 32, 128), bf16),
-        v((R, 32, 128), bf16),
-        v((R, 32, 128), bf16),
-        v((R, 32, 128), bf16),
+        v((R, 1, 32, 128), bf16),
+        v((1, R, 32, 128), bf16),
+        v((R, 1, 32, 128), bf16),
+        v((1, R, 32, 128), bf16),
         v((288, WW), bf16),
         v((256, 256), bf16),
         v((128, 256), bf16),
@@ -598,8 +625,8 @@
         v((320, 128), f32),
         v((16, 512), bf16),
     ]
-    one, by_x = [dma((1,))] * 2, [dma((2,))] * 2
-    sems = [dma((15,))] + by_x + by_x + one + [dma((3,))] * 3 + one + by_x + by_x + one + one
+    one, two, four = [dma((1,))] * 2, [dma((2,))] * 2, [dma((4,))] * 2
+    sems = [dma((15,))] + two * 3 + [dma((3,))] * 3 + two * 2 + four + one * 2
     return buffers + sems
 
 

time: 74.1 us -> 81.6 us (1.10)
  Pallas kernels: 72.5 us -> 80 us
    pallas_call x1, Pallas kernels: 72.5 us -> 80 us  [local(): pl.pallas_call(kernel, out_shape=jax.ShapeDtypeStruct((100, 128), bf16),...]
where the time goes in v7:
time: 81.6 us; the launch traced here: 81.3 us
  Pallas kernels  80 us (98%)
  local copies, waits for them, and re-layouts  1.35 us (2%)
    pallas_call x1, Pallas kernels, local(): pl.pallas_call(kernel, out_shape=jax.ShapeDtypeStruct((100, 128), bf16),...  80 us

profile of v7, /device:TPU:1, one launch (start us, length us, event | category | flops | bytes accessed | tf_op | source)
XLA Modules:
  0.0 81.3 jit_solution(13356920434637698600)
XLA Ops:
  0.0 80.0 %shard_map.217 = bf16[100,128]{1,0:T(8,128)(2,1)} custom-call(bf16[2,320,1024]{2,1,0:T(8,128)(2,1)} %bitcast.11, bf16[3,3,18,800]{3,2,1,0:T(8,128)(2,1)} %bitcast.12, bf16[20,20]{1,0:T(8,128)(2,1)} %refs_2_.1, f32[1,20]{1,0:T(1,128)} %bitcast.16, bf16[20,64]{1,0:T(8,128)(2,1)} %refs_4_.1, f32[1,64]{1,0:T(1,128)} %bitcast.17, bf16[1,64]{1,0:T(2,128)(2,1)} %bitcast.18, ...), custom_call_target="tpu_custom_call" | custom-call | tf_op jit(solution)/shard_map/pallas_call | solution.py:660
  80.0 1.4 %copy.25 = bf16[1,1,100,128]{3,2,1,0:T(8,128)(2,1)} copy(bf16[1,1,100,128]{3,2,1,0:T(8,128)(2,1)} %bitcast.13) | data formatting | bytes 51200

commit v8 on v6

--- a/solution.py
+++ b/solution.py
@@ -166,11 +166,6 @@
         jx, jy = lax.div(first, MY), lax.rem(first, MY)
         sources.append((R * zh + lax.div(jy, 3), lax.rem(jx, 3)))
 
-    barrier = pltpu.get_barrier_semaphore()
-    for near in (on_y, on_z, on_e):
-        for d in range(1, R):
-            pl.semaphore_signal(barrier, inc=1, device_id=near(d)[1], device_id_type=MESH)
-
     fetch = []
     wanted = [
         (t_fwd_in, t_fwd), (field_in.at[0], field.at[0]), (field_in.at[1], field.at[1]),
@@ -181,7 +176,16 @@
     ]
     for n, (source, target) in enumerate(wanted):
         fetch.append(pltpu.make_async_copy(source, target, fetched.at[n]))
-        fetch[n].start()
+    for copy in fetch[:3]:
+        copy.start()
+
+    barrier = pltpu.get_barrier_semaphore()
+    for near in (on_y, on_z, on_e):
+        for d in range(1, R):
+            pl.semaphore_signal(barrier, inc=1, device_id=near(d)[1], device_id_type=MESH)
+
+    for copy in fetch[3:]:
+        copy.start()
 
     sent = []
 
@@ -273,7 +277,7 @@
 
         for view, sem in sent:
             await_bytes(view, sem)
-        for recv, send_sem in ((recv_y, ss_y), (recv_a, ss_a), (recv_d, ss_d), (recv_e, ss_e)):
+        for recv, send_sem in ((recv_y, ss_y), (recv_a, ss_a), (recv_e, ss_e)):
             for x in range(2):
                 await_bytes(recv.at[x, pl.ds(0, R - 1)], send_sem.at[x])
 
@@ -481,11 +485,11 @@
     for x in range(2):
         for p in range(R):
             send_d[p, x] = xd[48 * p + 24 * x : 48 * p + 24 * x + 24, :].astype(bf16)
-        start_e(x, send_d, recv_d, ss_d, rs_d)
+    exchange(on_e, e, send_d, recv_d, ss_d, rs_d)
 
     for x in range(2):
-        finish_y(x, recv_d, rs_d)
-        xe[...] = recv_d[x].astype(f32).reshape(192, 128)
+        for p in range(R):
+            xe[24 * p : 24 * p + 24, :] = recv_d[p, x].astype(f32)
         data = jnp.concatenate(
             [by_frequency(xe, lambda m: G * m + g, 24) for g in range(G)], axis=1
         ).astype(bf16)
@@ -524,9 +528,9 @@
             value = mm(s6[...], t_bwd[:, cut]) + mm(skip_k[...], field[x, :, cut])
             halves = value.reshape(C, 2, 8, 256)
             for h in range(2):
-                state = twice_gelu(halves[:, h].reshape(160, 256).astype(bf16))
+                state = twice_gelu(halves[:, h].reshape(160, 256)).astype(bf16)
                 state = jnp.concatenate([state, jnp.ones((16, 256), bf16)], axis=0)
-                hidden = twice_gelu(mm(hid_k[...], state).astype(bf16))
+                hidden = twice_gelu(mm(hid_k[...], state)).astype(bf16)
                 part[pl.ds(pl.multiple_of(x * 16, 16) + 8 * h, 8), cut] = mm(out_k[...], hidden)[0:8]
 
     for b in range(8):
@@ -577,7 +581,7 @@
         v((448, 128), f32),
         v((384, 128), f32),
         v((R, 2, 24, 128), bf16),
-        v((2, R, 24, 128), bf16),
+        v((R, 2, 24, 128), bf16),
         v((192, 128), f32),
         v((R, 2, 16, LW), bf16),
         v((2, R, 16, LW), bf16),
@@ -599,7 +603,7 @@
         v((16, 512), bf16),
     ]
     one, by_x = [dma((1,))] * 2, [dma((2,))] * 2
-    sems = [dma((15,))] + by_x + by_x + one + [dma((3,))] * 3 + one + by_x + by_x + one + one
+    sems = [dma((15,))] + by_x + by_x + one + [dma((3,))] * 3 + one + one + by_x + one + one
     return buffers + sems
 
 

time: 74.1 us -> 74.6 us (level)
  no operation moved by 1% of the time
where the time goes in v8:
time: 74.6 us; the launch traced here: 74.1 us
  Pallas kernels  72.8 us (98%)
  local copies, waits for them, and re-layouts  1.35 us (2%)
    pallas_call x1, Pallas kernels, local(): pl.pallas_call(kernel, out_shape=jax.ShapeDtypeStruct((100, 128), bf16),...  72.8 us

profile of v8, /device:TPU:1, one launch (start us, length us, event | category | flops | bytes accessed | tf_op | source)
XLA Modules:
  0.0 74.1 jit_solution(8525307192009738734)
XLA Ops:
  0.0 72.8 %shard_map.217 = bf16[100,128]{1,0:T(8,128)(2,1)} custom-call(bf16[2,320,1024]{2,1,0:T(8,128)(2,1)} %bitcast.11, bf16[3,3,18,800]{3,2,1,0:T(8,128)(2,1)} %bitcast.12, bf16[20,20]{1,0:T(8,128)(2,1)} %refs_2_.1, f32[1,20]{1,0:T(1,128)} %bitcast.16, bf16[20,64]{1,0:T(8,128)(2,1)} %refs_4_.1, f32[1,64]{1,0:T(1,128)} %bitcast.17, bf16[1,64]{1,0:T(2,128)(2,1)} %bitcast.18, ...), custom_call_target="tpu_custom_call" | custom-call | tf_op jit(solution)/shard_map/pallas_call | solution.py:637
  72.8 1.4 %copy.25 = bf16[1,1,100,128]{3,2,1,0:T(8,128)(2,1)} copy(bf16[1,1,100,128]{3,2,1,0:T(8,128)(2,1)} %bitcast.13) | data formatting | bytes 51200

commit v9 on v8

--- a/solution.py
+++ b/solution.py
@@ -133,7 +133,7 @@
         widen, widen_sw, sum_re, sum_im, regroup,
         send_y, recv_y, ya, send_a, recv_a, xa, xb, send_b, recv_b,
         pairs, amat, mix, send_c, recv_c, xc, xd, send_d, recv_d, xe, send_e, recv_e,
-        s6, part, blk, send_f, recv_f, send_g, recv_g, wpad, perm, pick, idrows, square, skip_k, hid_k,
+        s6, skipped, part, blk, send_f, recv_f, send_g, recv_g, wpad, perm, pick, idrows, square, skip_k, hid_k,
         skip_bias, out_k,
         fetched,
         ss_y, rs_y, ss_a, rs_a, ss_b, rs_b, ss_p, rs_p, ls_p, ss_c, rs_c,
@@ -462,6 +462,10 @@
     send_c[...] = mix[...].astype(bf16)
 
     def prepare_late():
+        for x in range(2):
+            for c in range(4):
+                cut = slice(256 * c, 256 * c + 256)
+                skipped[x, :, cut] = mm(skip_k[...], field[x, :, cut])
         prepare_out()
         prepare_rows()
 
@@ -525,7 +529,7 @@
 
         for c in range(4):
             cut = slice(256 * c, 256 * c + 256)
-            value = mm(s6[...], t_bwd[:, cut]) + mm(skip_k[...], field[x, :, cut])
+            value = mm(s6[...], t_bwd[:, cut]) + skipped[x, :, cut]
             halves = value.reshape(C, 2, 8, 256)
             for h in range(2):
                 state = twice_gelu(halves[:, h].reshape(160, 256)).astype(bf16)
@@ -539,10 +543,9 @@
     send_f[...] = mm(perm[...], blk[...].astype(bf16)).astype(bf16).reshape(R, 32, 128)
     exchange(on_z, zh, send_f, recv_f, ss_f, rs_f)
     send_g[...] = mm(regroup[...], recv_f[...].reshape(256, 128)).astype(bf16).reshape(R, 32, 128)
-    exchange(on_e, e, send_g, recv_g, ss_g, rs_g)
+    exchange(on_e, e, send_g, recv_g, ss_g, rs_g, beside=finish_sends)
     owned = mm(pick[...], recv_g[...].reshape(256, 128))
     out[...] = owned[0:100].astype(bf16)
-    finish_sends()
 
 
 def scratch():
@@ -586,6 +589,7 @@
         v((R, 2, 16, LW), bf16),
         v((2, R, 16, LW), bf16),
         v((320, 384), bf16),
+        v((2, 320, 1024), f32),
         v((32, 1024), f32),
         v((256, 128), f32),
         v((R, 32, 128), bf16),

time: 74.6 us -> 73.8 us (0.989)
  Pallas kernels: 72.8 us -> 72 us
    pallas_call x1, Pallas kernels: 72.8 us -> 72 us  [local(): pl.pallas_call(kernel, out_shape=jax.ShapeDtypeStruct((100, 128), bf16),...]
where the time goes in v9:
time: 73.8 us; the launch traced here: 73.4 us
  Pallas kernels  72 us (98%)
  local copies, waits for them, and re-layouts  1.35 us (2%)
    pallas_call x1, Pallas kernels, local(): pl.pallas_call(kernel, out_shape=jax.ShapeDtypeStruct((100, 128), bf16),...  72 us

profile of v9, /device:TPU:1, one launch (start us, length us, event | category | flops | bytes accessed | tf_op | source)
XLA Modules:
  0.0 73.4 jit_solution(14339077275746197118)
XLA Ops:
  0.0 72.0 %shard_map.217 = bf16[100,128]{1,0:T(8,128)(2,1)} custom-call(bf16[2,320,1024]{2,1,0:T(8,128)(2,1)} %bitcast.11, bf16[3,3,18,800]{3,2,1,0:T(8,128)(2,1)} %bitcast.12, bf16[20,20]{1,0:T(8,128)(2,1)} %refs_2_.1, f32[1,20]{1,0:T(1,128)} %bitcast.16, bf16[20,64]{1,0:T(8,128)(2,1)} %refs_4_.1, f32[1,64]{1,0:T(1,128)} %bitcast.17, bf16[1,64]{1,0:T(2,128)(2,1)} %bitcast.18, ...), custom_call_target="tpu_custom_call" | custom-call | tf_op jit(solution)/shard_map/pallas_call | solution.py:641
  72.0 1.4 %copy.25 = bf16[1,1,100,128]{3,2,1,0:T(8,128)(2,1)} copy(bf16[1,1,100,128]{3,2,1,0:T(8,128)(2,1)} %bitcast.13) | data formatting | bytes 51200

commit v10 on v9

--- a/solution.py
+++ b/solution.py
@@ -323,10 +323,10 @@
     along_zt(0)
     pl.semaphore_wait(barrier, 3 * (R - 1))
     start_y(0, send_y, recv_y, ss_y, rs_y)
-    start_weights()
     fetch[2].wait()
     along_zt(1)
     start_y(1, send_y, recv_y, ss_y, rs_y)
+    start_weights()
     for copy in fetch[3:]:
         copy.wait()
 

time: 73.8 us -> 74.6 us (1.011)
  Pallas kernels: 72 us -> 73 us
    pallas_call x1, Pallas kernels: 72 us -> 73 us  [local(): pl.pallas_call(kernel, out_shape=jax.ShapeDtypeStruct((100, 128), bf16),...]
where the time goes in v10:
time: 74.6 us; the launch traced here: 74.4 us
  Pallas kernels  73 us (98%)
  local copies, waits for them, and re-layouts  1.35 us (2%)
    pallas_call x1, Pallas kernels, local(): pl.pallas_call(kernel, out_shape=jax.ShapeDtypeStruct((100, 128), bf16),...  73 us

profile of v10, /device:TPU:1, one launch (start us, length us, event | category | flops | bytes accessed | tf_op | source)
XLA Modules:
  0.0 74.4 jit_solution(17063389031354352952)
XLA Ops:
  0.0 73.0 %shard_map.217 = bf16[100,128]{1,0:T(8,128)(2,1)} custom-call(bf16[2,320,1024]{2,1,0:T(8,128)(2,1)} %bitcast.11, bf16[3,3,18,800]{3,2,1,0:T(8,128)(2,1)} %bitcast.12, bf16[20,20]{1,0:T(8,128)(2,1)} %refs_2_.1, f32[1,20]{1,0:T(1,128)} %bitcast.16, bf16[20,64]{1,0:T(8,128)(2,1)} %refs_4_.1, f32[1,64]{1,0:T(1,128)} %bitcast.17, bf16[1,64]{1,0:T(2,128)(2,1)} %bitcast.18, ...), custom_call_target="tpu_custom_call" | custom-call | tf_op jit(solution)/shard_map/pallas_call | solution.py:641
  73.0 1.4 %copy.25 = bf16[1,1,100,128]{3,2,1,0:T(8,128)(2,1)} copy(bf16[1,1,100,128]{3,2,1,0:T(8,128)(2,1)} %bitcast.13) | data formatting | bytes 51200
